TPU v7x, 32 devices: a whole 2x2x4 slice. The times are simulated.
32 devices in a mesh: grp: 4 (over y, core), lane: 8 (over z, x).
Axes of the slice: x: 2, y: 2, z: 4, core: 2. Of those that a mesh axis runs over, the one named last changes fastest.
Arguments:
- fine_in: bfloat16 [2, 512, 16, 256], P(None, ('grp', 'lane')), may hold values from -6 to 6
- counts: int32 [2, 32], P(None, ('grp', 'lane')), may hold values from 1 to 15, as said below
- neighbour_refs: int32 [2, 512, 16], P(None, ('grp', 'lane')), may hold values from 0 to 79, as said below
- offset_codes: int32 [2, 512, 16], P(None, ('grp', 'lane')), may hold values from 0 to 26, as said below
- neighbour_mask: int32 [2, 512, 16], P(None, ('grp', 'lane')), may hold values 0 or 1
- send_slots: int32 [2, 32, 64], P(None, ('grp', 'lane')), may hold values from 0 to 14, as said below
- parent_of: int32 [512], P(('grp', 'lane')), may hold values from -1 to 7, as said below
- child_code: int32 [512], P(('grp', 'lane')), may hold values from 0 to 7, as said below
- coarse_refs: int32 [32, 16], P(('grp', 'lane')), may hold values from 0 to 31
- coarse_codes: int32 [32, 16], P(('grp', 'lane')), may hold values from 0 to 26, as said below
- coarse_mask: int32 [32, 16], P(('grp', 'lane')), may hold values 0 or 1
- ops_x: bfloat16 [3, 4, 3, 16, 16], replicated, may hold values from -0.75 to 0.75
- ops_y: bfloat16 [3, 4, 3, 16, 16], replicated, may hold values from -0.75 to 0.75
- ops_z: bfloat16 [3, 4, 3, 16, 16], replicated, may hold values from -0.75 to 0.75
- filters: bfloat16 [2, 16, 16], replicated, may hold values from -1.5 to 1.5
Outputs:
- fine_out: bfloat16 [2, 512, 16, 256], P(None, ('grp', 'lane'))
- coarse_out: bfloat16 [32, 16, 256], P(('grp', 'lane'))
Inputs may be any that keep to these rules, and one draw needn't show every extreme that they name: The counts of the devices of one grp index add up to 64 on level 1. send_slots[l, q, r * 2 + c] is a live slot of device q on level l. `neighbour_refs`: A value below 16 is a live slot of the block's own device; a larger one is 16 + q * 2 + c, entry c of what device q sends to the block's device. `offset_codes`: the codes of one block are distinct. `coarse_codes`: the codes of one coarse block are distinct. `parent_of`: -1 exactly on slots that are not live on level 1; every coarse block of a subtree has 8 live children there, one of each child code. `child_code`: 0 on slots that are not live.
All inputs are finite; a program needn't handle non-finite values. No bound on the sum of `neighbour_mask` or of `coarse_mask` on one device may be relied on, other than what follows from the above.
Results may differ from a plain program's by a relative error of at most 0.0088.
Values may be sent and summed in bfloat16 or wider, within the bound.
A program may use at most 256 MiB of HBM per device.

v0:
```python
import functools

import jax
import jax.numpy as jnp
from jax import lax
from jax.experimental import pallas as pl
from jax.experimental.pallas import tpu as pltpu
from jax.sharding import PartitionSpec as P

MESH = pl.DeviceIdType.MESH
BF = jnp.bfloat16
F32 = jnp.float32
OFFSETS = 27
PLANES = 9
GROUP = 4


def dot_nn(a, b):
    return jnp.dot(a, b, preferred_element_type=F32)


def dot_nt(a, b):
    return lax.dot_general(a, b, (((1,), (1,)), ((), ())), preferred_element_type=F32)


def one_hot(shape, fn):
    rows = lax.broadcasted_iota(jnp.int32, shape, 0)
    cols = lax.broadcasted_iota(jnp.int32, shape, 1)
    return jnp.where(fn(rows, cols), 1.0, 0.0).astype(BF)


def spread_first(k):
    return one_hot((k, k * k), lambda i, j: (j >= i * k) & (j < i * k + k))


def spread_second(k):
    return one_hot((k, k * k), lambda i, j: lax.rem(j, k) == i)


def kron_rows(left, right, k):
    return jnp.concatenate([(left[p : p + 1, :] * right).astype(BF) for p in range(k)], axis=0)


def build_filters(filters_ref, hk_ref, k):
    first, second = spread_first(k), spread_second(k)
    left = [dot_nn(filters_ref[c], first) for c in range(2)]
    right = [dot_nn(filters_ref[c], second) for c in range(2)]
    for cy in range(2):
        for cz in range(2):
            hk_ref[2 * cy + cz] = kron_rows(left[cy], right[cz], k)


def build_tables(level, ops_y_ref, ops_z_ref, kr_ref, k, terms):
    first, second = spread_first(k), spread_second(k)

    def one_term(m, carry):
        right = [dot_nn(ops_z_ref[level, m, c], second) for c in range(3)]
        for cy in range(3):
            left = dot_nn(ops_y_ref[level, m, cy], first)
            for cz in range(3):
                kr_ref[m * PLANES + 3 * cy + cz] = kron_rows(left, right[cz], k)
        return carry

    lax.fori_loop(0, terms, one_term, 0)


def build_rows(level, ops_x_ref, group, k, terms):
    width = group * 3 * k
    blocks = []
    stacked = [
        jnp.concatenate([ops_x_ref[level, m, c] for m in range(terms)], axis=0) for c in range(3)
    ]
    for g in range(group):
        total = None
        for c in range(3):
            offset = (g * 3 + c) * k
            part = dot_nn(stacked[c], one_hot((k, width), lambda i, j: j == i + offset))
            total = part if total is None else total + part
        blocks.append(total.astype(BF))
    return jnp.concatenate(
        [blocks[g][m * k : (m + 1) * k] for m in range(terms) for g in range(group)], axis=0
    )


def spread_group(base, group, rows_mat, load, s_ref, k, terms):
    for plane in range(PLANES):
        source = jnp.concatenate(
            [load(base + g, 9 * c + plane) for g in range(group) for c in range(3)], axis=0
        )
        out = dot_nn(rows_mat, source).astype(BF)
        span = group * k
        for m in range(terms):
            s_ref[m * PLANES + plane, pl.ds(base * k, span), :] = out[m * span : (m + 1) * span]


def apply_tables(s_ref, kr_ref, rows, k, terms):
    def one_term(m, total):
        for plane in range(PLANES):
            at = m * PLANES + plane
            total = total + dot_nt(s_ref[at, pl.ds(0, rows), :], kr_ref[at])
        return total

    return lax.fori_loop(0, terms, one_term, jnp.zeros((rows, k * k), F32))


def comm_kernel(
    dims,
    fine_ref,
    slots_ref,
    parent_ref,
    child_ref,
    cidx_ref,
    ops_x_ref,
    ops_y_ref,
    ops_z_ref,
    filters_ref,
    pool_out,
    group_out,
    coarse_out,
    pool,
    outgoing,
    partial,
    rs_buf,
    coarse_all,
    group_all,
    hk,
    kr,
    s_buf,
    wide,
    send_rs,
    recv_rs,
    send_ag,
    recv_ag,
    send_co,
    recv_co,
    send_fine,
    recv_fine,
):
    n_grp, n_lane, cap, slot, par_lane, k, terms = dims
    n_dev = n_grp * n_lane
    grp = lax.axis_index("grp")
    lane = lax.axis_index("lane")
    me = grp * n_lane + lane

    def coords(d):
        return (lax.div(d, n_lane), lax.rem(d, n_lane))

    barrier = pltpu.get_barrier_semaphore()

    def greet(i, carry):
        pl.semaphore_signal(
            barrier, inc=1, device_id=coords(lax.rem(me + i, n_dev)), device_id_type=MESH
        )
        return carry

    lax.fori_loop(1, n_dev, greet, 0)

    build_filters(filters_ref, hk, k)
    both = jnp.concatenate([filters_ref[0], filters_ref[1]], axis=0)
    for b in range(slot):
        lifted = dot_nn(both, fine_ref[1, b])
        code = child_ref[b]
        upper = code >= 4
        corner = jnp.where(upper, code - 4, code)
        chosen = jnp.where(upper, lifted[k:], lifted[:k])
        for c in range(4):
            wide[c, b * k : (b + 1) * k, :] = jnp.where(corner == c, chosen, 0.0).astype(BF)
    terms_up = dot_nt(wide[0], hk[0])
    for c in range(1, 4):
        terms_up = terms_up + dot_nt(wide[c], hk[c])
    for t in range(n_lane * par_lane):
        total = jnp.zeros((k, k * k), F32)
        for b in range(slot):
            total = total + jnp.where(parent_ref[b] == t, terms_up[b * k : (b + 1) * k], 0.0)
        partial[t // par_lane, t % par_lane] = total

    def gather(d, carry):
        for level in range(2):
            for c in range(cap):
                outgoing[level, d, c] = fine_ref[level, slots_ref[level, 0, d * cap + c]]
        return carry

    lax.fori_loop(0, n_dev, gather, 0)
    pl.semaphore_wait(barrier, n_dev - 1)

    def send_partial(i, carry):
        to = lax.rem(lane + i, n_lane)
        pltpu.make_async_remote_copy(
            src_ref=partial.at[to],
            dst_ref=rs_buf.at[lane],
            send_sem=send_rs,
            recv_sem=recv_rs,
            device_id=(grp, to),
            device_id_type=MESH,
        ).start()
        return carry

    lax.fori_loop(1, n_lane, send_partial, 0)

    def send_fine_level(level):
        def one(i, carry):
            d = lax.rem(me + i, n_dev)
            pltpu.make_async_remote_copy(
                src_ref=outgoing.at[level, d],
                dst_ref=pool.at[level, pl.ds(slot + me * cap, cap)],
                send_sem=send_fine.at[level],
                recv_sem=recv_fine.at[level],
                device_id=coords(d),
                device_id_type=MESH,
            ).start()
            return carry

        lax.fori_loop(1, n_dev, one, 0)

    rs_buf[lane] = partial[lane]
    for level in range(2):
        pool[level, pl.ds(0, slot)] = fine_ref[level]
        pool[level, pl.ds(slot + me * cap, cap)] = outgoing[level, me]
        pool[level, slot + n_dev * cap] = jnp.zeros((k, k * k), BF)
    coarse_all[n_dev * par_lane] = jnp.zeros((k, k * k), BF)
    build_tables(2, ops_y_ref, ops_z_ref, kr, k, terms)
    rows_mat = build_rows(2, ops_x_ref, 1, k, terms)

    def await_bytes(ref, sem):
        pltpu.make_async_copy(ref, ref, sem).wait()

    await_bytes(rs_buf.at[pl.ds(0, n_lane - 1)], recv_rs)
    total = rs_buf[0]
    for t in range(1, n_lane):
        total = total + rs_buf[t]
    coarse_all[pl.ds(me * par_lane, par_lane)] = total.astype(BF)

    def send_coarse(i, carry):
        d = lax.rem(me + i, n_dev)
        mine = coarse_all.at[pl.ds(me * par_lane, par_lane)]
        pltpu.make_async_remote_copy(
            src_ref=mine,
            dst_ref=mine,
            send_sem=send_ag,
            recv_sem=recv_ag,
            device_id=coords(d),
            device_id_type=MESH,
        ).start()
        return carry

    lax.fori_loop(1, n_dev, send_coarse, 0)
    send_fine_level(0)
    send_fine_level(1)
    await_bytes(coarse_all.at[pl.ds(0, (n_dev - 1) * par_lane)], recv_ag)

    for b in range(par_lane):
        spread_group(
            b, 1, rows_mat, lambda i, code: coarse_all[cidx_ref[i, code]], s_buf, k, terms
        )
    result = apply_tables(s_buf, kr, par_lane * k, k, terms).astype(BF)
    for b in range(par_lane):
        group_all[lane, b] = result[b * k : (b + 1) * k]
        coarse_out[b] = result[b * k : (b + 1) * k]

    def send_result(i, carry):
        to = lax.rem(lane + i, n_lane)
        pltpu.make_async_remote_copy(
            src_ref=group_all.at[lane],
            dst_ref=group_all.at[lane],
            send_sem=send_co,
            recv_sem=recv_co,
            device_id=(grp, to),
            device_id_type=MESH,
        ).start()
        return carry

    lax.fori_loop(1, n_lane, send_result, 0)
    await_bytes(group_all.at[pl.ds(0, n_lane - 1)], recv_co)
    group_out[...] = group_all[...]
    for level in range(2):
        await_bytes(pool.at[level, pl.ds(0, (n_dev - 1) * cap)], recv_fine.at[level])
    pool_out[...] = pool[...]
    await_bytes(rs_buf.at[pl.ds(0, n_lane - 1)], send_rs)
    await_bytes(coarse_all.at[pl.ds(0, (n_dev - 1) * par_lane)], send_ag)
    await_bytes(group_all.at[pl.ds(0, n_lane - 1)], send_co)
    for level in range(2):
        await_bytes(pool.at[level, pl.ds(0, (n_dev - 1) * cap)], send_fine.at[level])


def fine_kernel(
    dims,
    pool,
    group_all,
    idx_ref,
    counts_ref,
    parent_ref,
    child_ref,
    ops_x_ref,
    ops_y_ref,
    ops_z_ref,
    filters_ref,
    out_ref,
    hk,
    kr,
    s_buf,
    wide,
):
    n_grp, n_lane, cap, slot, par_lane, k, terms = dims
    build_filters(filters_ref, hk, k)
    correction = drop(group_all, parent_ref, child_ref, filters_ref, hk, wide, slot, par_lane, k)
    for level in range(2):
        build_tables(level, ops_y_ref, ops_z_ref, kr, k, terms)
        result = fine_operator(level, pool, idx_ref, ops_x_ref, kr, s_buf, slot, k, terms)
        for b in range(slot):
            value = jnp.where(b < counts_ref[level, 0], result[b * k : (b + 1) * k], 0.0)
            if level == 1:
                value = value + correction[b * k : (b + 1) * k]
            out_ref[level, b] = value.astype(BF)


def fine_operator(level, pool, idx_ref, ops_x_ref, kr, s_buf, slot, k, terms):
    group = GROUP if slot % GROUP == 0 else 1
    rows_mat = build_rows(level, ops_x_ref, group, k, terms)

    def one_group(g, carry):
        spread_group(
            pl.multiple_of(g * group, group),
            group,
            rows_mat,
            lambda i, code: pool[level, idx_ref[level, i, code]],
            s_buf,
            k,
            terms,
        )
        return carry

    lax.fori_loop(0, slot // group, one_group, 0)
    return apply_tables(s_buf, kr, slot * k, k, terms)


def drop(group_all, parent_ref, child_ref, filters_ref, hk, wide, slot, par_lane, k):
    eye = one_hot((k, k), lambda i, j: i == j)
    both = jnp.concatenate([dot_nt(eye, filters_ref[c]).astype(BF) for c in range(2)], axis=0)
    for b in range(slot):
        parent = parent_ref[b]
        held = jnp.maximum(parent, 0)
        lowered = dot_nn(both, group_all[held])
        code = child_ref[b]
        upper = code >= 4
        corner = jnp.where(upper, code - 4, code)
        corner = jnp.where(parent >= 0, corner, -1)
        chosen = jnp.where(upper, lowered[k:], lowered[:k])
        for c in range(4):
            wide[c, b * k : (b + 1) * k, :] = jnp.where(corner == c, chosen, 0.0).astype(BF)
    total = dot_nn(wide[0], hk[0])
    for c in range(1, 4):
        total = total + dot_nn(wide[c], hk[c])
    return total


def code_table(refs, codes, mask, empty):
    hits = (
        codes[..., None, :] == jnp.arange(OFFSETS, dtype=jnp.int32)[:, None]
    ) & (mask[..., None, :] == 1)
    return empty + jnp.sum(jnp.where(hits, refs[..., None, :] - empty, 0), axis=-1)


def body(
    fine_in,
    counts,
    neighbour_refs,
    offset_codes,
    neighbour_mask,
    send_slots,
    parent_of,
    child_code,
    coarse_refs,
    coarse_codes,
    coarse_mask,
    ops_x,
    ops_y,
    ops_z,
    filters,
):
    n_grp, n_lane = lax.axis_size("grp"), lax.axis_size("lane")
    n_dev = n_grp * n_lane
    k = filters.shape[1]
    kk = k * k
    slot = fine_in.shape[1]
    cap = send_slots.shape[2] // n_dev
    par_lane = coarse_refs.shape[0]
    terms = ops_x.shape[1]
    dims = (n_grp, n_lane, cap, slot, par_lane, k, terms)
    pool_size = slot + n_dev * cap + 1
    idx = code_table(neighbour_refs, offset_codes, neighbour_mask, slot + n_dev * cap)
    cidx = code_table(coarse_refs, coarse_codes, coarse_mask, n_dev * par_lane)
    vmem = pl.BlockSpec(memory_space=pltpu.VMEM)
    smem = pl.BlockSpec(memory_space=pltpu.SMEM)
    pool, group_all, coarse_out = pl.pallas_call(
        functools.partial(comm_kernel, dims),
        out_shape=(
            jax.ShapeDtypeStruct((2, pool_size, k, kk), BF),
            jax.ShapeDtypeStruct((n_lane, par_lane, k, kk), BF),
            jax.ShapeDtypeStruct((par_lane, k, kk), BF),
        ),
        in_specs=[vmem, smem, smem, smem, smem, vmem, vmem, vmem, vmem],
        out_specs=(vmem, vmem, vmem),
        scratch_shapes=[
            pltpu.VMEM((2, pool_size, k, kk), BF),
            pltpu.VMEM((2, n_dev, cap, k, kk), BF),
            pltpu.VMEM((n_lane, par_lane, k, kk), F32),
            pltpu.VMEM((n_lane, par_lane, k, kk), F32),
            pltpu.VMEM((n_dev * par_lane + 1, k, kk), BF),
            pltpu.VMEM((n_lane, par_lane, k, kk), BF),
            pltpu.VMEM((4, kk, kk), BF),
            pltpu.VMEM((terms * PLANES, kk, kk), BF),
            pltpu.VMEM((terms * PLANES, par_lane * k, kk), BF),
            pltpu.VMEM((4, slot * k, kk), BF),
            pltpu.SemaphoreType.DMA,
            pltpu.SemaphoreType.DMA,
            pltpu.SemaphoreType.DMA,
            pltpu.SemaphoreType.DMA,
            pltpu.SemaphoreType.DMA,
            pltpu.SemaphoreType.DMA,
            pltpu.SemaphoreType.DMA((2,)),
            pltpu.SemaphoreType.DMA((2,)),
        ],
        compiler_params=pltpu.CompilerParams(
            collective_id=0, has_side_effects=True, vmem_limit_bytes=48 * 1024 * 1024
        ),
    )(fine_in, send_slots, parent_of, child_code, cidx, ops_x, ops_y, ops_z, filters)
    fine_out = pl.pallas_call(
        functools.partial(fine_kernel, dims),
        out_shape=jax.ShapeDtypeStruct(fine_in.shape, BF),
        in_specs=[vmem, vmem, smem, smem, smem, smem, vmem, vmem, vmem, vmem],
        out_specs=vmem,
        scratch_shapes=[
            pltpu.VMEM((4, kk, kk), BF),
            pltpu.VMEM((terms * PLANES, kk, kk), BF),
            pltpu.VMEM((terms * PLANES, slot * k, kk), BF),
            pltpu.VMEM((4, slot * k, kk), BF),
        ],
        compiler_params=pltpu.CompilerParams(vmem_limit_bytes=48 * 1024 * 1024),
    )(
        pool,
        group_all.reshape(n_lane * par_lane, k, kk),
        idx,
        counts,
        parent_of,
        child_code,
        ops_x,
        ops_y,
        ops_z,
        filters,
    )
    return fine_out, coarse_out


def solution(mesh):
    both = ("grp", "lane")
    in_specs = (
        P(None, both, None, None),
        P(None, both),
        P(None, both, None),
        P(None, both, None),
        P(None, both, None),
        P(None, both, None),
        P(both),
        P(both),
        P(both, None),
        P(both, None),
        P(both, None),
        P(),
        P(),
        P(),
        P(),
    )
    out_specs = (P(None, both, None, None), P(both, None, None))
    return jax.shard_map(body, mesh=mesh, in_specs=in_specs, out_specs=out_specs, check_vma=False)
```

profile of v0, /device:TPU:0, one launch (start us, length us, event | category | flops | bytes accessed | tf_op | source)
XLA Modules:
  0.0 72.2 jit_solution(17895727289870944425)
XLA Ops:
  0.6 0.7 add_bitcast_fusion.1
  1.3 0.7 compare_bitcast_fusion
  1.9 0.7 %select_reduce_fusion.1 = s32[27]{0:T(128)S(1)} fusion(s32[16]{0:T(128)S(1)} %add_bitcast_fusion.1, s32[16]{0:T(128)} %bitcast.9, pred[16]{0:T(512)(128)(4,1)S(1)} %compare_bitcast_fusion), kind=kLoop, calls=%fused_computation.6 | loop fusion | flops 1701 | bytes 252 | tf_op jit(solution)/shard_map/reduce_sum | solution.py:360
  2.7 0.7 %copy.18.counts_ref = s32[2,1]{1,0:T(2,128)S(1)} copy(s32[2,1]{0,1:T(1,128)} %param.16) | data formatting | bytes 16 | tf_op args[1]
  3.4 0.7 broadcast_compare_fusion
  4.2 0.7 broadcast_add_fusion.1
  4.9 1.0 %select_reduce_fusion = s32[2,16,27]{2,1,0:T(8,128)S(1)} fusion(s32[2,16,16]{2,1,0:T(8,128)S(1)} %broadcast_add_fusion.1, s32[2,16,16]{2,1,0:T(8,128)} %param.18, pred[2,16,16]{2,1,0:T(8,128)(4,1)S(1)} %broadcast_compare_fusion), kind=kLoop, calls=%fused_computation | loop fusion | flops 54432 | bytes 8064 | tf_op jit(solution)/shard_map/reduce_sum | solution.py:360
  5.9 0.0 copy-start
  5.9 0.9 %copy-done = bf16[3,4,3,16,16]{4,3,2,1,0:T(8,128)(2,1)S(1)} copy-done((bf16[3,4,3,16,16]{4,3,2,1,0:T(8,128)(2,1)S(1)}, bf16[3,4,3,16,16]{4,3,2,1,0:T(8,128)(2,1)}, u32[]{:S(2)}) %copy-start) | copy-done | bytes 18456
  6.8 0.0 copy-start.2
  6.8 0.9 %copy-done.2 = bf16[3,4,3,16,16]{4,3,2,1,0:T(8,128)(2,1)S(1)} copy-done((bf16[3,4,3,16,16]{4,3,2,1,0:T(8,128)(2,1)S(1)}, bf16[3,4,3,16,16]{4,3,2,1,0:T(8,128)(2,1)}, u32[]{:S(2)}) %copy-start.2) | copy-done | bytes 18456
  7.7 0.0 copy-start.4
  7.7 0.9 %copy-done.4 = bf16[3,4,3,16,16]{4,3,2,1,0:T(8,128)(2,1)S(1)} copy-done((bf16[3,4,3,16,16]{4,3,2,1,0:T(8,128)(2,1)S(1)}, bf16[3,4,3,16,16]{4,3,2,1,0:T(8,128)(2,1)}, u32[]{:S(2)}) %copy-start.4) | copy-done | bytes 18456
  8.6 0.0 copy-start.5
  8.6 0.9 %copy-done.5 = bf16[2,16,16,256]{3,2,1,0:T(8,128)(2,1)S(1)} copy-done((bf16[2,16,16,256]{3,2,1,0:T(8,128)(2,1)S(1)}, bf16[2,16,16,256]{3,2,1,0:T(8,128)(2,1)}, u32[]{:S(2)}) %copy-start.5) | copy-done | bytes 262168
  9.6 0.0 copy-start.6
  9.6 0.7 copy-done.6
  10.3 0.0 copy-start.7
  10.3 0.7 copy-done.7
  10.9 0.0 copy-start.9
  10.9 0.7 copy-done.9
  11.6 0.0 copy-start.11
  11.6 0.7 copy-done.11
  12.3 43.7 %shard_map.158 = (bf16[2,81,16,256]{3,2,1,0:T(8,128)(2,1)S(1)}, bf16[8,1,16,256]{3,2,1,0:T(8,128)(2,1)S(1)}, bf16[1,16,256]{2,1,0:T(8,128)(2,1)S(1)}) custom-call(bf16[2,16,16,256]{3,2,1,0:T(8,128)(2,1)S(1)} %copy-done.5, s32[2,1,64]{2,1,0:T(1,128)S(1)} %copy-done.11, s32[16]{0:T(128)S(1)} %copy-done.7, s32[16]{0:T(128)S(1)} %copy-done.9, ...), custom_call_target="tpu_custom_call" | custom-call | tf_op jit(solution)/shard_map/pallas_call | solution.py:394
  56.0 0.0 copy-start.1
  56.0 0.9 %copy-done.1 = bf16[3,4,3,16,16]{4,3,2,1,0:T(8,128)(2,1)S(1)} copy-done((bf16[3,4,3,16,16]{4,3,2,1,0:T(8,128)(2,1)S(1)}, bf16[3,4,3,16,16]{4,3,2,1,0:T(8,128)(2,1)}, u32[]{:S(2)}) %copy-start.1) | copy-done | bytes 18456
  56.9 0.0 copy-start.3
  56.9 0.9 %copy-done.3 = bf16[3,4,3,16,16]{4,3,2,1,0:T(8,128)(2,1)S(1)} copy-done((bf16[3,4,3,16,16]{4,3,2,1,0:T(8,128)(2,1)S(1)}, bf16[3,4,3,16,16]{4,3,2,1,0:T(8,128)(2,1)}, u32[]{:S(2)}) %copy-start.3) | copy-done | bytes 18456
  57.8 0.0 copy-start.8
  57.8 0.7 copy-done.8
  58.5 0.0 copy-start.10
  58.5 0.7 copy-done.10
  59.1 12.5 %shard_map.159 = bf16[2,16,16,256]{3,2,1,0:T(8,128)(2,1)} custom-call(bf16[2,81,16,256]{3,2,1,0:T(8,128)(2,1)S(1)} %get-tuple-element.5.pool, bf16[8,16,256]{2,1,0:T(8,128)(2,1)S(1)} %bitcast.8, s32[2,16,27]{2,1,0:T(8,128)S(1)} %broadcast_add_fusion.idx_ref, s32[2,1]{1,0:T(2,128)S(1)} %copy.18.counts_ref, s32[16]{0:T(128)S(1)} %copy-done.8, ...), custom_call_target="tpu_custom_call" | custom-call | tf_op jit(solution)/shard_map/pallas_call | solution.py:427
  71.6 0.6 copy.20
  (2 shorter events, 0.0 us)
Async XLA Ops:
  5.9 0.9 %copy-start = (bf16[3,4,3,16,16]{4,3,2,1,0:T(8,128)(2,1)S(1)}, bf16[3,4,3,16,16]{4,3,2,1,0:T(8,128)(2,1)}, u32[]{:S(2)}) copy-start(bf16[3,4,3,16,16]{4,3,2,1,0:T(8,128)(2,1)} %ops_x_ref.3) | copy-start | bytes 55300
  6.8 0.9 %copy-start.2 = (bf16[3,4,3,16,16]{4,3,2,1,0:T(8,128)(2,1)S(1)}, bf16[3,4,3,16,16]{4,3,2,1,0:T(8,128)(2,1)}, u32[]{:S(2)}) copy-start(bf16[3,4,3,16,16]{4,3,2,1,0:T(8,128)(2,1)} %ops_y_ref.3) | copy-start | bytes 55300
  7.7 0.9 %copy-start.4 = (bf16[3,4,3,16,16]{4,3,2,1,0:T(8,128)(2,1)S(1)}, bf16[3,4,3,16,16]{4,3,2,1,0:T(8,128)(2,1)}, u32[]{:S(2)}) copy-start(bf16[3,4,3,16,16]{4,3,2,1,0:T(8,128)(2,1)} %ops_z_ref.3) | copy-start | bytes 55300
  8.6 0.9 %copy-start.5 = (bf16[2,16,16,256]{3,2,1,0:T(8,128)(2,1)S(1)}, bf16[2,16,16,256]{3,2,1,0:T(8,128)(2,1)}, u32[]{:S(2)}) copy-start(bf16[2,16,16,256]{3,2,1,0:T(8,128)(2,1)} %fine_ref.1) | copy-start | bytes 786436
  9.6 0.7 copy-start.6
  10.3 0.7 copy-start.7
  10.9 0.7 copy-start.9
  11.6 0.7 copy-start.11
  56.0 0.9 %copy-start.1 = (bf16[3,4,3,16,16]{4,3,2,1,0:T(8,128)(2,1)S(1)}, bf16[3,4,3,16,16]{4,3,2,1,0:T(8,128)(2,1)}, u32[]{:S(2)}) copy-start(bf16[3,4,3,16,16]{4,3,2,1,0:T(8,128)(2,1)} %ops_x_ref.3) | copy-start | bytes 55300
  56.9 0.9 %copy-start.3 = (bf16[3,4,3,16,16]{4,3,2,1,0:T(8,128)(2,1)S(1)}, bf16[3,4,3,16,16]{4,3,2,1,0:T(8,128)(2,1)}, u32[]{:S(2)}) copy-start(bf16[3,4,3,16,16]{4,3,2,1,0:T(8,128)(2,1)} %ops_y_ref.3) | copy-start | bytes 55300
  57.8 0.7 copy-start.8
  58.5 0.7 copy-start.10
where the time goes:
time: 72.8 us; the launch traced here: 72.2 us
  Pallas kernels  56.2 us (77%)
  local copies, waits for them, and re-layouts  10.8 us (15%)
  other arithmetic  4.51 us (6%)
    pallas_call x1, Pallas kernels, body(): pl.pallas_call(functools.partial(comm_kernel, dims), out_shape=(jax.Shape...  43.7 us
    pallas_call x1, Pallas kernels, body(): pl.pallas_call(functools.partial(fine_kernel, dims), out_shape=jax.ShapeD...  12.5 us
    unnamed x26, local copies, waits for them, and re-layouts  10.8 us
    reduce_sum x2, other arithmetic, code_table(): jnp.sum(jnp.where(hits, refs[..., None, :] - empty, 0), axis=-1)  1.74 us

commit v1 on v0

--- a/solution.py
+++ b/solution.py
@@ -103,21 +103,57 @@
     return lax.fori_loop(0, terms, one_term, jnp.zeros((rows, k * k), F32))
 
 
-def comm_kernel(
+def fill_index(refs, codes, mask, empty, out_ref, at):
+    rows, slots = refs.shape
+    code_of = lax.broadcasted_iota(jnp.int32, (rows, 128), 1)
+    total = jnp.full((rows, 128), empty, jnp.int32)
+    for j in range(slots):
+        hit = (codes[:, j : j + 1] == code_of) & (mask[:, j : j + 1] == 1)
+        total = jnp.where(hit, refs[:, j : j + 1], total)
+    out_ref[at] = total
+
+
+def tree_kernel(
     dims,
-    fine_ref,
+    fine_hbm,
+    counts_hbm,
+    refs_hbm,
+    codes_hbm,
+    mask_hbm,
+    slots_hbm,
+    parent_hbm,
+    child_hbm,
+    crefs_hbm,
+    ccodes_hbm,
+    cmask_hbm,
+    ops_x_hbm,
+    ops_y_hbm,
+    ops_z_hbm,
+    filters_hbm,
+    out_ref,
+    coarse_out,
+    counts_ref,
+    refs_ref,
+    codes_ref,
+    mask_ref,
     slots_ref,
     parent_ref,
     child_ref,
-    cidx_ref,
+    crefs_ref,
+    ccodes_ref,
+    cmask_ref,
     ops_x_ref,
     ops_y_ref,
     ops_z_ref,
     filters_ref,
-    pool_out,
-    group_out,
-    coarse_out,
-    pool,
+    idx_vec,
+    cidx_vec,
+    idx_ref,
+    cidx_ref,
+    own_0,
+    own_1,
+    pool_0,
+    pool_1,
     outgoing,
     partial,
     rs_buf,
@@ -127,6 +163,7 @@
     kr,
     s_buf,
     wide,
+    in_sems,
     send_rs,
     recv_rs,
     send_ag,
@@ -138,12 +175,39 @@
 ):
     n_grp, n_lane, cap, slot, par_lane, k, terms = dims
     n_dev = n_grp * n_lane
+    own, pool = (own_0, own_1), (pool_0, pool_1)
     grp = lax.axis_index("grp")
     lane = lax.axis_index("lane")
     me = grp * n_lane + lane
 
     def coords(d):
         return (lax.div(d, n_lane), lax.rem(d, n_lane))
+
+    fetches = [
+        pltpu.make_async_copy(src, dst, in_sems.at[i])
+        for i, (src, dst) in enumerate(
+            [
+                (filters_hbm, filters_ref),
+                (fine_hbm.at[1], own_1),
+                (child_hbm, child_ref),
+                (parent_hbm, parent_ref),
+                (slots_hbm, slots_ref),
+                (fine_hbm.at[0], own_0),
+                (crefs_hbm, crefs_ref),
+                (ccodes_hbm, ccodes_ref),
+                (cmask_hbm, cmask_ref),
+                (ops_x_hbm, ops_x_ref),
+                (ops_y_hbm, ops_y_ref),
+                (ops_z_hbm, ops_z_ref),
+                (refs_hbm, refs_ref),
+                (codes_hbm, codes_ref),
+                (mask_hbm, mask_ref),
+                (counts_hbm, counts_ref),
+            ]
+        )
+    ]
+    for fetch in fetches:
+        fetch.start()
 
     barrier = pltpu.get_barrier_semaphore()
 
@@ -155,10 +219,12 @@
 
     lax.fori_loop(1, n_dev, greet, 0)
 
+    for fetch in fetches[:4]:
+        fetch.wait()
     build_filters(filters_ref, hk, k)
     both = jnp.concatenate([filters_ref[0], filters_ref[1]], axis=0)
     for b in range(slot):
-        lifted = dot_nn(both, fine_ref[1, b])
+        lifted = dot_nn(both, own_1[b])
         code = child_ref[b]
         upper = code >= 4
         corner = jnp.where(upper, code - 4, code)
@@ -173,14 +239,6 @@
         for b in range(slot):
             total = total + jnp.where(parent_ref[b] == t, terms_up[b * k : (b + 1) * k], 0.0)
         partial[t // par_lane, t % par_lane] = total
-
-    def gather(d, carry):
-        for level in range(2):
-            for c in range(cap):
-                outgoing[level, d, c] = fine_ref[level, slots_ref[level, 0, d * cap + c]]
-        return carry
-
-    lax.fori_loop(0, n_dev, gather, 0)
     pl.semaphore_wait(barrier, n_dev - 1)
 
     def send_partial(i, carry):
@@ -200,9 +258,11 @@
     def send_fine_level(level):
         def one(i, carry):
             d = lax.rem(me + i, n_dev)
+            for c in range(cap):
+                outgoing[level, d, c] = own[level][slots_ref[level, 0, d * cap + c]]
             pltpu.make_async_remote_copy(
                 src_ref=outgoing.at[level, d],
-                dst_ref=pool.at[level, pl.ds(slot + me * cap, cap)],
+                dst_ref=pool[level].at[pl.ds(slot + me * cap, cap)],
                 send_sem=send_fine.at[level],
                 recv_sem=recv_fine.at[level],
                 device_id=coords(d),
@@ -211,15 +271,30 @@
             return carry
 
         lax.fori_loop(1, n_dev, one, 0)
+        for c in range(cap):
+            pool[level][slot + me * cap + c] = own[level][slots_ref[level, 0, me * cap + c]]
+        pool[level][slot + n_dev * cap] = jnp.zeros((k, k * k), BF)
+        pool[level][pl.ds(0, slot)] = own[level][...]
+
+    for fetch in fetches[4:6]:
+        fetch.wait()
+    send_fine_level(0)
 
     rs_buf[lane] = partial[lane]
+    coarse_all[n_dev * par_lane] = jnp.zeros((k, k * k), BF)
+    for fetch in fetches[6:]:
+        fetch.wait()
+    fill_index(crefs_ref[...], ccodes_ref[...], cmask_ref[...], n_dev * par_lane, cidx_vec, ...)
     for level in range(2):
-        pool[level, pl.ds(0, slot)] = fine_ref[level]
-        pool[level, pl.ds(slot + me * cap, cap)] = outgoing[level, me]
-        pool[level, slot + n_dev * cap] = jnp.zeros((k, k * k), BF)
-    coarse_all[n_dev * par_lane] = jnp.zeros((k, k * k), BF)
-    build_tables(2, ops_y_ref, ops_z_ref, kr, k, terms)
-    rows_mat = build_rows(2, ops_x_ref, 1, k, terms)
+        fill_index(
+            refs_ref[level], codes_ref[level], mask_ref[level], slot + n_dev * cap, idx_vec, level
+        )
+    table_copies = [
+        pltpu.make_async_copy(cidx_vec, cidx_ref, in_sems.at[0]),
+        pltpu.make_async_copy(idx_vec, idx_ref, in_sems.at[1]),
+    ]
+    for copy in table_copies:
+        copy.start()
 
     def await_bytes(ref, sem):
         pltpu.make_async_copy(ref, ref, sem).wait()
@@ -244,15 +319,19 @@
         return carry
 
     lax.fori_loop(1, n_dev, send_coarse, 0)
-    send_fine_level(0)
     send_fine_level(1)
+    for level in (2, 0, 1):
+        build_tables(level, ops_y_ref, ops_z_ref, kr.at[level], k, terms)
+    rows_mat = build_rows(2, ops_x_ref, 1, k, terms)
+    for copy in table_copies:
+        copy.wait()
+
     await_bytes(coarse_all.at[pl.ds(0, (n_dev - 1) * par_lane)], recv_ag)
-
     for b in range(par_lane):
         spread_group(
             b, 1, rows_mat, lambda i, code: coarse_all[cidx_ref[i, code]], s_buf, k, terms
         )
-    result = apply_tables(s_buf, kr, par_lane * k, k, terms).astype(BF)
+    result = apply_tables(s_buf, kr.at[2], par_lane * k, k, terms).astype(BF)
     for b in range(par_lane):
         group_all[lane, b] = result[b * k : (b + 1) * k]
         coarse_out[b] = result[b * k : (b + 1) * k]
@@ -270,47 +349,28 @@
         return carry
 
     lax.fori_loop(1, n_lane, send_result, 0)
+
+    await_bytes(pool_0.at[pl.ds(0, (n_dev - 1) * cap)], recv_fine.at[0])
+    result = fine_operator(0, pool_0, idx_ref, ops_x_ref, kr.at[0], s_buf, slot, k, terms)
+    for b in range(slot):
+        value = jnp.where(b < counts_ref[0], result[b * k : (b + 1) * k], 0.0)
+        out_ref[0, b] = value.astype(BF)
+
     await_bytes(group_all.at[pl.ds(0, n_lane - 1)], recv_co)
-    group_out[...] = group_all[...]
-    for level in range(2):
-        await_bytes(pool.at[level, pl.ds(0, (n_dev - 1) * cap)], recv_fine.at[level])
-    pool_out[...] = pool[...]
+    correction = drop(
+        group_all, parent_ref, child_ref, filters_ref, hk, wide, slot, par_lane, k
+    )
+    await_bytes(pool_1.at[pl.ds(0, (n_dev - 1) * cap)], recv_fine.at[1])
+    result = fine_operator(1, pool_1, idx_ref, ops_x_ref, kr.at[1], s_buf, slot, k, terms)
+    for b in range(slot):
+        value = jnp.where(b < counts_ref[1], result[b * k : (b + 1) * k], 0.0)
+        out_ref[1, b] = (value + correction[b * k : (b + 1) * k]).astype(BF)
+
     await_bytes(rs_buf.at[pl.ds(0, n_lane - 1)], send_rs)
     await_bytes(coarse_all.at[pl.ds(0, (n_dev - 1) * par_lane)], send_ag)
     await_bytes(group_all.at[pl.ds(0, n_lane - 1)], send_co)
     for level in range(2):
-        await_bytes(pool.at[level, pl.ds(0, (n_dev - 1) * cap)], send_fine.at[level])
-
-
-def fine_kernel(
-    dims,
-    pool,
-    group_all,
-    idx_ref,
-    counts_ref,
-    parent_ref,
-    child_ref,
-    ops_x_ref,
-    ops_y_ref,
-    ops_z_ref,
-    filters_ref,
-    out_ref,
-    hk,
-    kr,
-    s_buf,
-    wide,
-):
-    n_grp, n_lane, cap, slot, par_lane, k, terms = dims
-    build_filters(filters_ref, hk, k)
-    correction = drop(group_all, parent_ref, child_ref, filters_ref, hk, wide, slot, par_lane, k)
-    for level in range(2):
-        build_tables(level, ops_y_ref, ops_z_ref, kr, k, terms)
-        result = fine_operator(level, pool, idx_ref, ops_x_ref, kr, s_buf, slot, k, terms)
-        for b in range(slot):
-            value = jnp.where(b < counts_ref[level, 0], result[b * k : (b + 1) * k], 0.0)
-            if level == 1:
-                value = value + correction[b * k : (b + 1) * k]
-            out_ref[level, b] = value.astype(BF)
+        await_bytes(pool[level].at[pl.ds(0, (n_dev - 1) * cap)], send_fine.at[level])
 
 
 def fine_operator(level, pool, idx_ref, ops_x_ref, kr, s_buf, slot, k, terms):
@@ -322,7 +382,7 @@
             pl.multiple_of(g * group, group),
             group,
             rows_mat,
-            lambda i, code: pool[level, idx_ref[level, i, code]],
+            lambda i, code: pool[idx_ref[level, i, code]],
             s_buf,
             k,
             terms,
@@ -339,7 +399,7 @@
     for b in range(slot):
         parent = parent_ref[b]
         held = jnp.maximum(parent, 0)
-        lowered = dot_nn(both, group_all[held])
+        lowered = dot_nn(both, group_all[held // par_lane, held % par_lane] if par_lane > 1 else group_all[held, 0])
         code = child_ref[b]
         upper = code >= 4
         corner = jnp.where(upper, code - 4, code)
@@ -351,13 +411,6 @@
     for c in range(1, 4):
         total = total + dot_nn(wide[c], hk[c])
     return total
-
-
-def code_table(refs, codes, mask, empty):
-    hits = (
-        codes[..., None, :] == jnp.arange(OFFSETS, dtype=jnp.int32)[:, None]
-    ) & (mask[..., None, :] == 1)
-    return empty + jnp.sum(jnp.where(hits, refs[..., None, :] - empty, 0), axis=-1)
 
 
 def body(
@@ -387,68 +440,80 @@
     terms = ops_x.shape[1]
     dims = (n_grp, n_lane, cap, slot, par_lane, k, terms)
     pool_size = slot + n_dev * cap + 1
-    idx = code_table(neighbour_refs, offset_codes, neighbour_mask, slot + n_dev * cap)
-    cidx = code_table(coarse_refs, coarse_codes, coarse_mask, n_dev * par_lane)
+    int32 = jnp.int32
     vmem = pl.BlockSpec(memory_space=pltpu.VMEM)
-    smem = pl.BlockSpec(memory_space=pltpu.SMEM)
-    pool, group_all, coarse_out = pl.pallas_call(
-        functools.partial(comm_kernel, dims),
+    hbm = pl.BlockSpec(memory_space=pl.ANY)
+    dma = pltpu.SemaphoreType.DMA
+    return pl.pallas_call(
+        functools.partial(tree_kernel, dims),
         out_shape=(
-            jax.ShapeDtypeStruct((2, pool_size, k, kk), BF),
-            jax.ShapeDtypeStruct((n_lane, par_lane, k, kk), BF),
+            jax.ShapeDtypeStruct(fine_in.shape, BF),
             jax.ShapeDtypeStruct((par_lane, k, kk), BF),
         ),
-        in_specs=[vmem, smem, smem, smem, smem, vmem, vmem, vmem, vmem],
-        out_specs=(vmem, vmem, vmem),
+        in_specs=[hbm] * 15,
+        out_specs=(vmem, vmem),
         scratch_shapes=[
-            pltpu.VMEM((2, pool_size, k, kk), BF),
+            pltpu.SMEM((2,), int32),
+            pltpu.VMEM(neighbour_refs.shape, int32),
+            pltpu.VMEM(offset_codes.shape, int32),
+            pltpu.VMEM(neighbour_mask.shape, int32),
+            pltpu.SMEM(send_slots.shape, int32),
+            pltpu.SMEM(parent_of.shape, int32),
+            pltpu.SMEM(child_code.shape, int32),
+            pltpu.VMEM(coarse_refs.shape, int32),
+            pltpu.VMEM(coarse_codes.shape, int32),
+            pltpu.VMEM(coarse_mask.shape, int32),
+            pltpu.VMEM(ops_x.shape, BF),
+            pltpu.VMEM(ops_y.shape, BF),
+            pltpu.VMEM(ops_z.shape, BF),
+            pltpu.VMEM(filters.shape, BF),
+            pltpu.VMEM((2, slot, 128), int32),
+            pltpu.VMEM((par_lane, 128), int32),
+            pltpu.SMEM((2, slot, 128), int32),
+            pltpu.SMEM((par_lane, 128), int32),
+            pltpu.VMEM((slot, k, kk), BF),
+            pltpu.VMEM((slot, k, kk), BF),
+            pltpu.VMEM((pool_size, k, kk), BF),
+            pltpu.VMEM((pool_size, k, kk), BF),
             pltpu.VMEM((2, n_dev, cap, k, kk), BF),
             pltpu.VMEM((n_lane, par_lane, k, kk), F32),
             pltpu.VMEM((n_lane, par_lane, k, kk), F32),
             pltpu.VMEM((n_dev * par_lane + 1, k, kk), BF),
             pltpu.VMEM((n_lane, par_lane, k, kk), BF),
             pltpu.VMEM((4, kk, kk), BF),
-            pltpu.VMEM((terms * PLANES, kk, kk), BF),
-            pltpu.VMEM((terms * PLANES, par_lane * k, kk), BF),
+            pltpu.VMEM((3, terms * PLANES, kk, kk), BF),
+            pltpu.VMEM((terms * PLANES, slot * k, kk), BF),
             pltpu.VMEM((4, slot * k, kk), BF),
-            pltpu.SemaphoreType.DMA,
-            pltpu.SemaphoreType.DMA,
-            pltpu.SemaphoreType.DMA,
-            pltpu.SemaphoreType.DMA,
-            pltpu.SemaphoreType.DMA,
-            pltpu.SemaphoreType.DMA,
-            pltpu.SemaphoreType.DMA((2,)),
-            pltpu.SemaphoreType.DMA((2,)),
+            dma((16,)),
+            dma,
+            dma,
+            dma,
+            dma,
+            dma,
+            dma,
+            dma((2,)),
+            dma((2,)),
         ],
         compiler_params=pltpu.CompilerParams(
-            collective_id=0, has_side_effects=True, vmem_limit_bytes=48 * 1024 * 1024
+            collective_id=0, has_side_effects=True, vmem_limit_bytes=56 * 1024 * 1024
         ),
-    )(fine_in, send_slots, parent_of, child_code, cidx, ops_x, ops_y, ops_z, filters)
-    fine_out = pl.pallas_call(
-        functools.partial(fine_kernel, dims),
-        out_shape=jax.ShapeDtypeStruct(fine_in.shape, BF),
-        in_specs=[vmem, vmem, smem, smem, smem, smem, vmem, vmem, vmem, vmem],
-        out_specs=vmem,
-        scratch_shapes=[
-            pltpu.VMEM((4, kk, kk), BF),
-            pltpu.VMEM((terms * PLANES, kk, kk), BF),
-            pltpu.VMEM((terms * PLANES, slot * k, kk), BF),
-            pltpu.VMEM((4, slot * k, kk), BF),
-        ],
-        compiler_params=pltpu.CompilerParams(vmem_limit_bytes=48 * 1024 * 1024),
     )(
-        pool,
-        group_all.reshape(n_lane * par_lane, k, kk),
-        idx,
-        counts,
+        fine_in,
+        counts.reshape(-1),
+        neighbour_refs,
+        offset_codes,
+        neighbour_mask,
+        send_slots,
         parent_of,
         child_code,
+        coarse_refs,
+        coarse_codes,
+        coarse_mask,
         ops_x,
         ops_y,
         ops_z,
         filters,
     )
-    return fine_out, coarse_out
 
 
 def solution(mesh):

time: 72.8 us -> 49.9 us (0.69)
  Pallas kernels: 56.2 us -> 46.8 us
  local copies, waits for them, and re-layouts: 10.8 us -> 2.28 us
  other arithmetic: 4.51 us -> 0 us
    pallas_call x2 -> x1, Pallas kernels: 56.2 us -> 46.8 us  [body(): pl.pallas_call(functools.partial(tree_kernel, dims), out_shape=(jax.Shape...]
    unnamed x26 -> x4, local copies, waits for them, and re-layouts: 10.8 us -> 2.28 us
    reduce_sum x2 -> x0, other arithmetic: 1.74 us -> none  [code_table(): jnp.sum(jnp.where(hits, refs[..., None, :] - empty, 0), axis=-1)]
    eq x2 -> x0, other arithmetic: 1.38 us -> none  [code_table(): mask[..., None, :] == 1]
    sub x2 -> x0, other arithmetic: 1.38 us -> none  [code_table(): refs[..., None, :] - empty]
where the time goes in v1:
time: 49.9 us; the launch traced here: 49.7 us
  Pallas kernels  46.8 us (94%)
  local copies, waits for them, and re-layouts  2.28 us (5%)
  between operations  0.65 us (1%)
    pallas_call x1, Pallas kernels, body(): pl.pallas_call(functools.partial(tree_kernel, dims), out_shape=(jax.Shape...  46.8 us
    unnamed x4, local copies, waits for them, and re-layouts  2.28 us

profile of v1, /device:TPU:0, one launch (start us, length us, event | category | flops | bytes accessed | tf_op | source)
XLA Modules:
  0.0 49.7 jit_solution(3796027489980970300)
XLA Ops:
  0.6 46.8 %shard_map.158 = (bf16[2,16,16,256]{3,2,1,0:T(8,128)(2,1)}, bf16[1,16,256]{2,1,0:T(8,128)(2,1)}) custom-call(bf16[2,16,16,256]{3,2,1,0:T(8,128)(2,1)} %fine_hbm.1, s32[2]{0:T(128)} %bitcast.1, s32[2,16,16]{2,1,0:T(8,128)} %refs_hbm.1, s32[2,16,16]{2,1,0:T(8,128)} %codes_hbm.1, s32[2,16,16]{2,1,0:T(8,128)} %mask_hbm.1, s32[2,1,64]{2,1,0:T(1,128)} %slots_hbm.1, ...), custom_call_target="tpu_custom_call" | custom-call | tf_op jit(solution)/shard_map/pallas_call | solution.py:447
  47.4 0.0 copy-start
  47.4 1.7 %copy.19 = bf16[2,16,16,256]{3,2,1,0:T(8,128)(2,1)} copy(bf16[2,16,16,256]{3,2,1,0:T(8,128)(2,1)} %get-tuple-element.4) | data formatting | bytes 524288
  49.1 0.0 copy-done
  49.1 0.6 %copy.20 = bf16[1,16,256]{2,1,0:T(8,128)(2,1)} copy(bf16[1,16,256]{2,1,0:T(8,128)(2,1)S(1)} %copy-done) | data formatting | bytes 16384
Async XLA Ops:
  47.4 1.7 %copy-start = (bf16[1,16,256]{2,1,0:T(8,128)(2,1)S(1)}, bf16[1,16,256]{2,1,0:T(8,128)(2,1)}, u32[]{:S(2)}) copy-start(bf16[1,16,256]{2,1,0:T(8,128)(2,1)} %get-tuple-element.5) | copy-start | bytes 24580

commit v2 on v1

--- a/solution.py
+++ b/solution.py
@@ -52,13 +52,19 @@
 
 def build_tables(level, ops_y_ref, ops_z_ref, kr_ref, k, terms):
     first, second = spread_first(k), spread_second(k)
+    eye = one_hot((k, k), lambda i, j: i == j)
+    kk = k * k
+
+    def turned(matrix):
+        return dot_nt(eye, matrix).astype(BF)
 
     def one_term(m, carry):
-        right = [dot_nn(ops_z_ref[level, m, c], second) for c in range(3)]
+        right = [dot_nn(turned(ops_z_ref[level, m, c]), second) for c in range(3)]
         for cy in range(3):
-            left = dot_nn(ops_y_ref[level, m, cy], first)
+            left = dot_nn(turned(ops_y_ref[level, m, cy]), first)
             for cz in range(3):
-                kr_ref[m * PLANES + 3 * cy + cz] = kron_rows(left, right[cz], k)
+                at = (3 * cy + cz) * kk
+                kr_ref[m, at : at + kk, :] = kron_rows(left, right[cz], k)
         return carry
 
     lax.fori_loop(0, terms, one_term, 0)
@@ -90,15 +96,14 @@
         out = dot_nn(rows_mat, source).astype(BF)
         span = group * k
         for m in range(terms):
-            s_ref[m * PLANES + plane, pl.ds(base * k, span), :] = out[m * span : (m + 1) * span]
+            s_ref[m, pl.ds(base * k, span), plane * k * k : (plane + 1) * k * k] = out[
+                m * span : (m + 1) * span
+            ]
 
 
 def apply_tables(s_ref, kr_ref, rows, k, terms):
     def one_term(m, total):
-        for plane in range(PLANES):
-            at = m * PLANES + plane
-            total = total + dot_nt(s_ref[at, pl.ds(0, rows), :], kr_ref[at])
-        return total
+        return total + dot_nn(s_ref[m, pl.ds(0, rows), :], kr_ref[m])
 
     return lax.fori_loop(0, terms, one_term, jnp.zeros((rows, k * k), F32))
 
@@ -168,9 +173,11 @@
     recv_rs,
     send_ag,
     recv_ag,
+    send_pass,
+    recv_pass,
     send_co,
     recv_co,
-    send_fine,
+    send_fine_sem,
     recv_fine,
 ):
     n_grp, n_lane, cap, slot, par_lane, k, terms = dims
@@ -183,16 +190,24 @@
     def coords(d):
         return (lax.div(d, n_lane), lax.rem(d, n_lane))
 
+    barrier = pltpu.get_barrier_semaphore()
+
+    def greet(i, carry):
+        pl.semaphore_signal(
+            barrier, inc=1, device_id=coords(lax.rem(me + i, n_dev)), device_id_type=MESH
+        )
+        return carry
+
     fetches = [
         pltpu.make_async_copy(src, dst, in_sems.at[i])
         for i, (src, dst) in enumerate(
             [
+                (slots_hbm, slots_ref),
+                (fine_hbm.at[0], own_0),
                 (filters_hbm, filters_ref),
                 (fine_hbm.at[1], own_1),
                 (child_hbm, child_ref),
                 (parent_hbm, parent_ref),
-                (slots_hbm, slots_ref),
-                (fine_hbm.at[0], own_0),
                 (crefs_hbm, crefs_ref),
                 (ccodes_hbm, ccodes_ref),
                 (cmask_hbm, cmask_ref),
@@ -208,18 +223,43 @@
     ]
     for fetch in fetches:
         fetch.start()
-
-    barrier = pltpu.get_barrier_semaphore()
-
-    def greet(i, carry):
-        pl.semaphore_signal(
-            barrier, inc=1, device_id=coords(lax.rem(me + i, n_dev)), device_id_type=MESH
-        )
-        return carry
-
     lax.fori_loop(1, n_dev, greet, 0)
 
-    for fetch in fetches[:4]:
+    def gather_level(level):
+        def one(d, carry):
+            for c in range(cap):
+                outgoing[level, d, c] = own[level][slots_ref[level, 0, d * cap + c]]
+            return carry
+
+        lax.fori_loop(0, n_dev, one, 0)
+
+    def send_fine(level, start, stop):
+        def one(i, carry):
+            d = lax.rem(me + i, n_dev)
+            pltpu.make_async_remote_copy(
+                src_ref=outgoing.at[level, d],
+                dst_ref=pool[level].at[pl.ds(slot + me * cap, cap)],
+                send_sem=send_fine_sem.at[level],
+                recv_sem=recv_fine.at[level],
+                device_id=coords(d),
+                device_id_type=MESH,
+            ).start()
+            return carry
+
+        lax.fori_loop(start, stop, one, 0)
+
+    def keep_own(level):
+        pool[level][pl.ds(slot + me * cap, cap)] = outgoing[level, me]
+        pool[level][slot + n_dev * cap] = jnp.zeros((k, k * k), BF)
+        pool[level][pl.ds(0, slot)] = own[level][...]
+
+    for fetch in fetches[:2]:
+        fetch.wait()
+    gather_level(0)
+    pl.semaphore_wait(barrier, n_dev - 1)
+    send_fine(0, 1, n_dev)
+
+    for fetch in fetches[2:6]:
         fetch.wait()
     build_filters(filters_ref, hk, k)
     both = jnp.concatenate([filters_ref[0], filters_ref[1]], axis=0)
@@ -239,7 +279,6 @@
         for b in range(slot):
             total = total + jnp.where(parent_ref[b] == t, terms_up[b * k : (b + 1) * k], 0.0)
         partial[t // par_lane, t % par_lane] = total
-    pl.semaphore_wait(barrier, n_dev - 1)
 
     def send_partial(i, carry):
         to = lax.rem(lane + i, n_lane)
@@ -254,34 +293,13 @@
         return carry
 
     lax.fori_loop(1, n_lane, send_partial, 0)
-
-    def send_fine_level(level):
-        def one(i, carry):
-            d = lax.rem(me + i, n_dev)
-            for c in range(cap):
-                outgoing[level, d, c] = own[level][slots_ref[level, 0, d * cap + c]]
-            pltpu.make_async_remote_copy(
-                src_ref=outgoing.at[level, d],
-                dst_ref=pool[level].at[pl.ds(slot + me * cap, cap)],
-                send_sem=send_fine.at[level],
-                recv_sem=recv_fine.at[level],
-                device_id=coords(d),
-                device_id_type=MESH,
-            ).start()
-            return carry
-
-        lax.fori_loop(1, n_dev, one, 0)
-        for c in range(cap):
-            pool[level][slot + me * cap + c] = own[level][slots_ref[level, 0, me * cap + c]]
-        pool[level][slot + n_dev * cap] = jnp.zeros((k, k * k), BF)
-        pool[level][pl.ds(0, slot)] = own[level][...]
-
-    for fetch in fetches[4:6]:
-        fetch.wait()
-    send_fine_level(0)
+    gather_level(1)
+    send_fine(1, 1, n_dev // 2)
 
     rs_buf[lane] = partial[lane]
     coarse_all[n_dev * par_lane] = jnp.zeros((k, k * k), BF)
+    keep_own(0)
+    keep_own(1)
     for fetch in fetches[6:]:
         fetch.wait()
     fill_index(crefs_ref[...], ccodes_ref[...], cmask_ref[...], n_dev * par_lane, cidx_vec, ...)
@@ -295,6 +313,7 @@
     ]
     for copy in table_copies:
         copy.start()
+    build_tables(0, ops_y_ref, ops_z_ref, kr.at[0], k, terms)
 
     def await_bytes(ref, sem):
         pltpu.make_async_copy(ref, ref, sem).wait()
@@ -305,28 +324,49 @@
         total = total + rs_buf[t]
     coarse_all[pl.ds(me * par_lane, par_lane)] = total.astype(BF)
 
+    half = n_dev // 2
+    odd = lax.rem(grp, 2)
+    twin = grp + 1 - 2 * odd
+
     def send_coarse(i, carry):
-        d = lax.rem(me + i, n_dev)
+        at = lax.rem(lax.div(grp, 2) * n_lane + lane + i, half)
         mine = coarse_all.at[pl.ds(me * par_lane, par_lane)]
         pltpu.make_async_remote_copy(
             src_ref=mine,
             dst_ref=mine,
             send_sem=send_ag,
             recv_sem=recv_ag,
-            device_id=coords(d),
+            device_id=(2 * lax.div(at, n_lane) + odd, lax.rem(at, n_lane)),
             device_id_type=MESH,
         ).start()
         return carry
 
-    lax.fori_loop(1, n_dev, send_coarse, 0)
-    send_fine_level(1)
-    for level in (2, 0, 1):
+    lax.fori_loop(1, half, send_coarse, 0)
+    send_fine(1, n_dev // 2, n_dev)
+    for level in (2, 1):
         build_tables(level, ops_y_ref, ops_z_ref, kr.at[level], k, terms)
-    rows_mat = build_rows(2, ops_x_ref, 1, k, terms)
     for copy in table_copies:
         copy.wait()
 
-    await_bytes(coarse_all.at[pl.ds(0, (n_dev - 1) * par_lane)], recv_ag)
+    await_bytes(pool_0.at[pl.ds(0, (n_dev - 1) * cap)], recv_fine.at[0])
+    result = fine_operator(0, pool_0, idx_ref, ops_x_ref, kr.at[0], s_buf, slot, k, terms)
+    for b in range(slot):
+        value = jnp.where(b < counts_ref[0], result[b * k : (b + 1) * k], 0.0)
+        out_ref[0, b] = value.astype(BF)
+
+    await_bytes(coarse_all.at[pl.ds(0, (half - 1) * par_lane)], recv_ag)
+    for pair in range(n_grp // 2):
+        held = coarse_all.at[pl.ds((2 * pair + odd) * n_lane * par_lane, n_lane * par_lane)]
+        pltpu.make_async_remote_copy(
+            src_ref=held,
+            dst_ref=held,
+            send_sem=send_pass,
+            recv_sem=recv_pass,
+            device_id=(twin, lane),
+            device_id_type=MESH,
+        ).start()
+    rows_mat = build_rows(2, ops_x_ref, 1, k, terms)
+    await_bytes(coarse_all.at[pl.ds(0, half * par_lane)], recv_pass)
     for b in range(par_lane):
         spread_group(
             b, 1, rows_mat, lambda i, code: coarse_all[cidx_ref[i, code]], s_buf, k, terms
@@ -350,27 +390,22 @@
 
     lax.fori_loop(1, n_lane, send_result, 0)
 
-    await_bytes(pool_0.at[pl.ds(0, (n_dev - 1) * cap)], recv_fine.at[0])
-    result = fine_operator(0, pool_0, idx_ref, ops_x_ref, kr.at[0], s_buf, slot, k, terms)
-    for b in range(slot):
-        value = jnp.where(b < counts_ref[0], result[b * k : (b + 1) * k], 0.0)
-        out_ref[0, b] = value.astype(BF)
-
+    await_bytes(pool_1.at[pl.ds(0, (n_dev - 1) * cap)], recv_fine.at[1])
+    result = fine_operator(1, pool_1, idx_ref, ops_x_ref, kr.at[1], s_buf, slot, k, terms)
     await_bytes(group_all.at[pl.ds(0, n_lane - 1)], recv_co)
     correction = drop(
         group_all, parent_ref, child_ref, filters_ref, hk, wide, slot, par_lane, k
     )
-    await_bytes(pool_1.at[pl.ds(0, (n_dev - 1) * cap)], recv_fine.at[1])
-    result = fine_operator(1, pool_1, idx_ref, ops_x_ref, kr.at[1], s_buf, slot, k, terms)
     for b in range(slot):
         value = jnp.where(b < counts_ref[1], result[b * k : (b + 1) * k], 0.0)
         out_ref[1, b] = (value + correction[b * k : (b + 1) * k]).astype(BF)
 
     await_bytes(rs_buf.at[pl.ds(0, n_lane - 1)], send_rs)
-    await_bytes(coarse_all.at[pl.ds(0, (n_dev - 1) * par_lane)], send_ag)
+    await_bytes(coarse_all.at[pl.ds(0, (half - 1) * par_lane)], send_ag)
+    await_bytes(coarse_all.at[pl.ds(0, half * par_lane)], send_pass)
     await_bytes(group_all.at[pl.ds(0, n_lane - 1)], send_co)
     for level in range(2):
-        await_bytes(pool[level].at[pl.ds(0, (n_dev - 1) * cap)], send_fine.at[level])
+        await_bytes(pool[level].at[pl.ds(0, (n_dev - 1) * cap)], send_fine_sem.at[level])
 
 
 def fine_operator(level, pool, idx_ref, ops_x_ref, kr, s_buf, slot, k, terms):
@@ -481,10 +516,12 @@
             pltpu.VMEM((n_dev * par_lane + 1, k, kk), BF),
             pltpu.VMEM((n_lane, par_lane, k, kk), BF),
             pltpu.VMEM((4, kk, kk), BF),
-            pltpu.VMEM((3, terms * PLANES, kk, kk), BF),
-            pltpu.VMEM((terms * PLANES, slot * k, kk), BF),
+            pltpu.VMEM((3, terms, PLANES * kk, kk), BF),
+            pltpu.VMEM((terms, slot * k, PLANES * kk), BF),
             pltpu.VMEM((4, slot * k, kk), BF),
             dma((16,)),
+            dma,
+            dma,
             dma,
             dma,
             dma,

time: 49.9 us -> 45.7 us (0.916)
  Pallas kernels: 46.8 us -> 42.7 us
    pallas_call x1, Pallas kernels: 46.8 us -> 42.7 us  [body(): pl.pallas_call(functools.partial(tree_kernel, dims), out_shape=(jax.Shape...]
where the time goes in v2:
time: 45.7 us; the launch traced here: 45.6 us
  Pallas kernels  42.7 us (93%)
  local copies, waits for them, and re-layouts  2.28 us (5%)
  between operations  0.65 us (1%)
    pallas_call x1, Pallas kernels, body(): pl.pallas_call(functools.partial(tree_kernel, dims), out_shape=(jax.Shape...  42.7 us
    unnamed x4, local copies, waits for them, and re-layouts  2.28 us

profile of v2, /device:TPU:0, one launch (start us, length us, event | category | flops | bytes accessed | tf_op | source)
XLA Modules:
  0.0 45.6 jit_solution(6826133204221787292)
XLA Ops:
  0.6 42.7 %shard_map.158 = (bf16[2,16,16,256]{3,2,1,0:T(8,128)(2,1)}, bf16[1,16,256]{2,1,0:T(8,128)(2,1)}) custom-call(bf16[2,16,16,256]{3,2,1,0:T(8,128)(2,1)} %fine_hbm.1, s32[2]{0:T(128)} %bitcast.1, s32[2,16,16]{2,1,0:T(8,128)} %refs_hbm.1, s32[2,16,16]{2,1,0:T(8,128)} %codes_hbm.1, s32[2,16,16]{2,1,0:T(8,128)} %mask_hbm.1, s32[2,1,64]{2,1,0:T(1,128)} %slots_hbm.1, ...), custom_call_target="tpu_custom_call" | custom-call | tf_op jit(solution)/shard_map/pallas_call | solution.py:482
  43.3 0.0 copy-start
  43.3 1.7 %copy.19 = bf16[2,16,16,256]{3,2,1,0:T(8,128)(2,1)} copy(bf16[2,16,16,256]{3,2,1,0:T(8,128)(2,1)} %get-tuple-element.4) | data formatting | bytes 524288
  45.0 0.0 copy-done
  45.0 0.6 %copy.20 = bf16[1,16,256]{2,1,0:T(8,128)(2,1)} copy(bf16[1,16,256]{2,1,0:T(8,128)(2,1)S(1)} %copy-done) | data formatting | bytes 16384
Async XLA Ops:
  43.3 1.7 %copy-start = (bf16[1,16,256]{2,1,0:T(8,128)(2,1)S(1)}, bf16[1,16,256]{2,1,0:T(8,128)(2,1)}, u32[]{:S(2)}) copy-start(bf16[1,16,256]{2,1,0:T(8,128)(2,1)} %get-tuple-element.5) | copy-start | bytes 24580

commit v3 on v2

--- a/solution.py
+++ b/solution.py
@@ -159,7 +159,12 @@
     own_1,
     pool_0,
     pool_1,
-    outgoing,
+    packed_own,
+    packed_mate,
+    mate_0,
+    mate_1,
+    slots_vec,
+    mate_slots,
     partial,
     rs_buf,
     coarse_all,
@@ -179,10 +184,13 @@
     recv_co,
     send_fine_sem,
     recv_fine,
+    send_mate_sem,
+    recv_mate,
 ):
     n_grp, n_lane, cap, slot, par_lane, k, terms = dims
     n_dev = n_grp * n_lane
     own, pool = (own_0, own_1), (pool_0, pool_1)
+    mate_blocks = (mate_0, mate_1)
     grp = lax.axis_index("grp")
     lane = lax.axis_index("lane")
     me = grp * n_lane + lane
@@ -225,39 +233,68 @@
         fetch.start()
     lax.fori_loop(1, n_dev, greet, 0)
 
-    def gather_level(level):
-        def one(d, carry):
+    half = n_dev // 2
+    lane_half = n_lane // 2
+    side = lax.div(lane, lane_half)
+    mate_lane = lax.rem(lane + lane_half, n_lane)
+    mate = grp * n_lane + mate_lane
+    place = grp * lane_half + lane - side * lane_half
+
+    def peer(h):
+        return lax.div(h, lane_half), side * lane_half + lax.rem(h, lane_half)
+
+    def send_mate(src, dst, at):
+        pltpu.make_async_remote_copy(
+            src_ref=src,
+            dst_ref=dst,
+            send_sem=send_mate_sem.at[at],
+            recv_sem=recv_mate.at[at],
+            device_id=(grp, mate_lane),
+            device_id_type=MESH,
+        ).start()
+
+    def send_fine(level, owner, blocks, slots, packed):
+        def one(i, carry):
+            h = lax.rem(place + i, half)
+            to_grp, to_lane = peer(h)
+            d = to_grp * n_lane + to_lane
             for c in range(cap):
-                outgoing[level, d, c] = own[level][slots_ref[level, 0, d * cap + c]]
+                packed[level, h, c] = blocks[slots[level, 0, d * cap + c]]
+
+            @pl.when(i > 0)
+            def _():
+                pltpu.make_async_remote_copy(
+                    src_ref=packed.at[level, h],
+                    dst_ref=pool[level].at[pl.ds(slot + owner * cap, cap)],
+                    send_sem=send_fine_sem.at[level],
+                    recv_sem=recv_fine.at[level],
+                    device_id=(to_grp, to_lane),
+                    device_id_type=MESH,
+                ).start()
+
             return carry
 
-        lax.fori_loop(0, n_dev, one, 0)
-
-    def send_fine(level, start, stop):
-        def one(i, carry):
-            d = lax.rem(me + i, n_dev)
-            pltpu.make_async_remote_copy(
-                src_ref=outgoing.at[level, d],
-                dst_ref=pool[level].at[pl.ds(slot + me * cap, cap)],
-                send_sem=send_fine_sem.at[level],
-                recv_sem=recv_fine.at[level],
-                device_id=coords(d),
-                device_id_type=MESH,
-            ).start()
-            return carry
-
-        lax.fori_loop(start, stop, one, 0)
+        lax.fori_loop(0, half, one, 0)
+        pool[level][pl.ds(slot + owner * cap, cap)] = packed[level, place]
+
+    def pass_mate(level):
+        await_bytes(mate_blocks[level], recv_mate.at[level])
+        send_fine(level, mate, mate_blocks[level], mate_slots, packed_mate)
+
+    def await_bytes(ref, sem):
+        pltpu.make_async_copy(ref, ref, sem).wait()
 
     def keep_own(level):
-        pool[level][pl.ds(slot + me * cap, cap)] = outgoing[level, me]
         pool[level][slot + n_dev * cap] = jnp.zeros((k, k * k), BF)
         pool[level][pl.ds(0, slot)] = own[level][...]
 
+    pl.semaphore_wait(barrier, n_dev - 1)
+    send_mate(slots_hbm, slots_vec, 2)
+    send_mate(fine_hbm.at[0], mate_0, 0)
+    send_mate(fine_hbm.at[1], mate_1, 1)
     for fetch in fetches[:2]:
         fetch.wait()
-    gather_level(0)
-    pl.semaphore_wait(barrier, n_dev - 1)
-    send_fine(0, 1, n_dev)
+    send_fine(0, me, own_0, slots_ref, packed_own)
 
     for fetch in fetches[2:6]:
         fetch.wait()
@@ -293,8 +330,12 @@
         return carry
 
     lax.fori_loop(1, n_lane, send_partial, 0)
-    gather_level(1)
-    send_fine(1, 1, n_dev // 2)
+    await_bytes(slots_vec, recv_mate.at[2])
+    slots_copy = pltpu.make_async_copy(slots_vec, mate_slots, in_sems.at[2])
+    slots_copy.start()
+    slots_copy.wait()
+    pass_mate(0)
+    send_fine(1, me, own_1, slots_ref, packed_own)
 
     rs_buf[lane] = partial[lane]
     coarse_all[n_dev * par_lane] = jnp.zeros((k, k * k), BF)
@@ -315,16 +356,12 @@
         copy.start()
     build_tables(0, ops_y_ref, ops_z_ref, kr.at[0], k, terms)
 
-    def await_bytes(ref, sem):
-        pltpu.make_async_copy(ref, ref, sem).wait()
-
     await_bytes(rs_buf.at[pl.ds(0, n_lane - 1)], recv_rs)
     total = rs_buf[0]
     for t in range(1, n_lane):
         total = total + rs_buf[t]
     coarse_all[pl.ds(me * par_lane, par_lane)] = total.astype(BF)
 
-    half = n_dev // 2
     odd = lax.rem(grp, 2)
     twin = grp + 1 - 2 * odd
 
@@ -342,13 +379,13 @@
         return carry
 
     lax.fori_loop(1, half, send_coarse, 0)
-    send_fine(1, n_dev // 2, n_dev)
+    pass_mate(1)
     for level in (2, 1):
         build_tables(level, ops_y_ref, ops_z_ref, kr.at[level], k, terms)
     for copy in table_copies:
         copy.wait()
 
-    await_bytes(pool_0.at[pl.ds(0, (n_dev - 1) * cap)], recv_fine.at[0])
+    await_bytes(pool_0.at[pl.ds(0, (n_dev - 2) * cap)], recv_fine.at[0])
     result = fine_operator(0, pool_0, idx_ref, ops_x_ref, kr.at[0], s_buf, slot, k, terms)
     for b in range(slot):
         value = jnp.where(b < counts_ref[0], result[b * k : (b + 1) * k], 0.0)
@@ -390,7 +427,7 @@
 
     lax.fori_loop(1, n_lane, send_result, 0)
 
-    await_bytes(pool_1.at[pl.ds(0, (n_dev - 1) * cap)], recv_fine.at[1])
+    await_bytes(pool_1.at[pl.ds(0, (n_dev - 2) * cap)], recv_fine.at[1])
     result = fine_operator(1, pool_1, idx_ref, ops_x_ref, kr.at[1], s_buf, slot, k, terms)
     await_bytes(group_all.at[pl.ds(0, n_lane - 1)], recv_co)
     correction = drop(
@@ -405,7 +442,9 @@
     await_bytes(coarse_all.at[pl.ds(0, half * par_lane)], send_pass)
     await_bytes(group_all.at[pl.ds(0, n_lane - 1)], send_co)
     for level in range(2):
-        await_bytes(pool[level].at[pl.ds(0, (n_dev - 1) * cap)], send_fine_sem.at[level])
+        await_bytes(pool[level].at[pl.ds(0, (n_dev - 2) * cap)], send_fine_sem.at[level])
+        await_bytes(mate_blocks[level], send_mate_sem.at[level])
+    await_bytes(slots_vec, send_mate_sem.at[2])
 
 
 def fine_operator(level, pool, idx_ref, ops_x_ref, kr, s_buf, slot, k, terms):
@@ -510,7 +549,12 @@
             pltpu.VMEM((slot, k, kk), BF),
             pltpu.VMEM((pool_size, k, kk), BF),
             pltpu.VMEM((pool_size, k, kk), BF),
-            pltpu.VMEM((2, n_dev, cap, k, kk), BF),
+            pltpu.VMEM((2, n_dev // 2, cap, k, kk), BF),
+            pltpu.VMEM((2, n_dev // 2, cap, k, kk), BF),
+            pltpu.VMEM((slot, k, kk), BF),
+            pltpu.VMEM((slot, k, kk), BF),
+            pltpu.VMEM(send_slots.shape, int32),
+            pltpu.SMEM(send_slots.shape, int32),
             pltpu.VMEM((n_lane, par_lane, k, kk), F32),
             pltpu.VMEM((n_lane, par_lane, k, kk), F32),
             pltpu.VMEM((n_dev * par_lane + 1, k, kk), BF),
@@ -530,6 +574,8 @@
             dma,
             dma((2,)),
             dma((2,)),
+            dma((3,)),
+            dma((3,)),
         ],
         compiler_params=pltpu.CompilerParams(
             collective_id=0, has_side_effects=True, vmem_limit_bytes=56 * 1024 * 1024

time: 45.7 us -> 43.1 us (0.943)
  Pallas kernels: 42.7 us -> 40 us
    pallas_call x1, Pallas kernels: 42.7 us -> 40 us  [body(): pl.pallas_call(functools.partial(tree_kernel, dims), out_shape=(jax.Shape...]
where the time goes in v3:
time: 43.1 us; the launch traced here: 42.9 us
  Pallas kernels  40 us (93%)
  local copies, waits for them, and re-layouts  2.28 us (5%)
  between operations  0.65 us (2%)
    pallas_call x1, Pallas kernels, body(): pl.pallas_call(functools.partial(tree_kernel, dims), out_shape=(jax.Shape...  40 us
    unnamed x4, local copies, waits for them, and re-layouts  2.28 us

profile of v3, /device:TPU:0, one launch (start us, length us, event | category | flops | bytes accessed | tf_op | source)
XLA Modules:
  0.0 42.9 jit_solution(236358389253220307)
XLA Ops:
  0.6 40.0 %shard_map.158 = (bf16[2,16,16,256]{3,2,1,0:T(8,128)(2,1)}, bf16[1,16,256]{2,1,0:T(8,128)(2,1)}) custom-call(bf16[2,16,16,256]{3,2,1,0:T(8,128)(2,1)} %fine_hbm.1, s32[2]{0:T(128)} %bitcast.1, s32[2,16,16]{2,1,0:T(8,128)} %refs_hbm.1, s32[2,16,16]{2,1,0:T(8,128)} %codes_hbm.1, s32[2,16,16]{2,1,0:T(8,128)} %mask_hbm.1, s32[2,1,64]{2,1,0:T(1,128)} %slots_hbm.1, ...), custom_call_target="tpu_custom_call" | custom-call | tf_op jit(solution)/shard_map/pallas_call | solution.py:521
  40.7 0.0 copy-start
  40.7 1.7 %copy.19 = bf16[2,16,16,256]{3,2,1,0:T(8,128)(2,1)} copy(bf16[2,16,16,256]{3,2,1,0:T(8,128)(2,1)} %get-tuple-element.4) | data formatting | bytes 524288
  42.3 0.0 copy-done
  42.4 0.6 %copy.20 = bf16[1,16,256]{2,1,0:T(8,128)(2,1)} copy(bf16[1,16,256]{2,1,0:T(8,128)(2,1)S(1)} %copy-done) | data formatting | bytes 16384
Async XLA Ops:
  40.7 1.7 %copy-start = (bf16[1,16,256]{2,1,0:T(8,128)(2,1)S(1)}, bf16[1,16,256]{2,1,0:T(8,128)(2,1)}, u32[]{:S(2)}) copy-start(bf16[1,16,256]{2,1,0:T(8,128)(2,1)} %get-tuple-element.5) | copy-start | bytes 24580

commit v4 on v3

--- a/solution.py
+++ b/solution.py
@@ -37,17 +37,22 @@
     return one_hot((k, k * k), lambda i, j: lax.rem(j, k) == i)
 
 
-def kron_rows(left, right, k):
-    return jnp.concatenate([(left[p : p + 1, :] * right).astype(BF) for p in range(k)], axis=0)
+def row_copies(left, k):
+    return [jnp.broadcast_to(left[p : p + 1, :], left.shape).astype(BF) for p in range(k)]
+
+
+def kron_store(out_ref, rows, right, k):
+    for p in range(k):
+        out_ref[p * k : (p + 1) * k, :] = rows[p] * right
 
 
 def build_filters(filters_ref, hk_ref, k):
     first, second = spread_first(k), spread_second(k)
-    left = [dot_nn(filters_ref[c], first) for c in range(2)]
-    right = [dot_nn(filters_ref[c], second) for c in range(2)]
+    right = [dot_nn(filters_ref[c], second).astype(BF) for c in range(2)]
     for cy in range(2):
+        rows = row_copies(dot_nn(filters_ref[cy], first), k)
         for cz in range(2):
-            hk_ref[2 * cy + cz] = kron_rows(left[cy], right[cz], k)
+            kron_store(hk_ref.at[2 * cy + cz], rows, right[cz], k)
 
 
 def build_tables(level, ops_y_ref, ops_z_ref, kr_ref, k, terms):
@@ -59,12 +64,12 @@
         return dot_nt(eye, matrix).astype(BF)
 
     def one_term(m, carry):
-        right = [dot_nn(turned(ops_z_ref[level, m, c]), second) for c in range(3)]
+        right = [dot_nn(turned(ops_z_ref[level, m, c]), second).astype(BF) for c in range(3)]
         for cy in range(3):
-            left = dot_nn(turned(ops_y_ref[level, m, cy]), first)
+            rows = row_copies(dot_nn(turned(ops_y_ref[level, m, cy]), first), k)
             for cz in range(3):
                 at = (3 * cy + cz) * kk
-                kr_ref[m, at : at + kk, :] = kron_rows(left, right[cz], k)
+                kron_store(kr_ref.at[m, pl.ds(at, kk)], rows, right[cz], k)
         return carry
 
     lax.fori_loop(0, terms, one_term, 0)
@@ -210,6 +215,8 @@
         pltpu.make_async_copy(src, dst, in_sems.at[i])
         for i, (src, dst) in enumerate(
             [
+                (ops_y_hbm, ops_y_ref),
+                (ops_z_hbm, ops_z_ref),
                 (slots_hbm, slots_ref),
                 (fine_hbm.at[0], own_0),
                 (filters_hbm, filters_ref),
@@ -220,8 +227,6 @@
                 (ccodes_hbm, ccodes_ref),
                 (cmask_hbm, cmask_ref),
                 (ops_x_hbm, ops_x_ref),
-                (ops_y_hbm, ops_y_ref),
-                (ops_z_hbm, ops_z_ref),
                 (refs_hbm, refs_ref),
                 (codes_hbm, codes_ref),
                 (mask_hbm, mask_ref),
@@ -288,17 +293,23 @@
         pool[level][slot + n_dev * cap] = jnp.zeros((k, k * k), BF)
         pool[level][pl.ds(0, slot)] = own[level][...]
 
+    for fetch in fetches[:2]:
+        fetch.wait()
+    build_tables(2, ops_y_ref, ops_z_ref, kr.at[2], k, terms)
     pl.semaphore_wait(barrier, n_dev - 1)
     send_mate(slots_hbm, slots_vec, 2)
     send_mate(fine_hbm.at[0], mate_0, 0)
     send_mate(fine_hbm.at[1], mate_1, 1)
-    for fetch in fetches[:2]:
+    for fetch in fetches[2:4]:
         fetch.wait()
     send_fine(0, me, own_0, slots_ref, packed_own)
 
-    for fetch in fetches[2:6]:
+    for fetch in fetches[4:8]:
         fetch.wait()
     build_filters(filters_ref, hk, k)
+    await_bytes(slots_vec, recv_mate.at[2])
+    slots_copy = pltpu.make_async_copy(slots_vec, mate_slots, in_sems.at[2])
+    slots_copy.start()
     both = jnp.concatenate([filters_ref[0], filters_ref[1]], axis=0)
     for b in range(slot):
         lifted = dot_nn(both, own_1[b])
@@ -330,9 +341,6 @@
         return carry
 
     lax.fori_loop(1, n_lane, send_partial, 0)
-    await_bytes(slots_vec, recv_mate.at[2])
-    slots_copy = pltpu.make_async_copy(slots_vec, mate_slots, in_sems.at[2])
-    slots_copy.start()
     slots_copy.wait()
     pass_mate(0)
     send_fine(1, me, own_1, slots_ref, packed_own)
@@ -341,7 +349,7 @@
     coarse_all[n_dev * par_lane] = jnp.zeros((k, k * k), BF)
     keep_own(0)
     keep_own(1)
-    for fetch in fetches[6:]:
+    for fetch in fetches[8:]:
         fetch.wait()
     fill_index(crefs_ref[...], ccodes_ref[...], cmask_ref[...], n_dev * par_lane, cidx_vec, ...)
     for level in range(2):
@@ -380,16 +388,9 @@
 
     lax.fori_loop(1, half, send_coarse, 0)
     pass_mate(1)
-    for level in (2, 1):
-        build_tables(level, ops_y_ref, ops_z_ref, kr.at[level], k, terms)
+    build_tables(1, ops_y_ref, ops_z_ref, kr.at[1], k, terms)
     for copy in table_copies:
         copy.wait()
-
-    await_bytes(pool_0.at[pl.ds(0, (n_dev - 2) * cap)], recv_fine.at[0])
-    result = fine_operator(0, pool_0, idx_ref, ops_x_ref, kr.at[0], s_buf, slot, k, terms)
-    for b in range(slot):
-        value = jnp.where(b < counts_ref[0], result[b * k : (b + 1) * k], 0.0)
-        out_ref[0, b] = value.astype(BF)
 
     await_bytes(coarse_all.at[pl.ds(0, (half - 1) * par_lane)], recv_ag)
     for pair in range(n_grp // 2):
@@ -402,6 +403,13 @@
             device_id=(twin, lane),
             device_id_type=MESH,
         ).start()
+
+    await_bytes(pool_0.at[pl.ds(0, (n_dev - 2) * cap)], recv_fine.at[0])
+    result = fine_operator(0, pool_0, idx_ref, ops_x_ref, kr.at[0], s_buf, slot, k, terms)
+    for b in range(slot):
+        value = jnp.where(b < counts_ref[0], result[b * k : (b + 1) * k], 0.0)
+        out_ref[0, b] = value.astype(BF)
+
     rows_mat = build_rows(2, ops_x_ref, 1, k, terms)
     await_bytes(coarse_all.at[pl.ds(0, half * par_lane)], recv_pass)
     for b in range(par_lane):
@@ -521,8 +529,8 @@
     return pl.pallas_call(
         functools.partial(tree_kernel, dims),
         out_shape=(
-            jax.ShapeDtypeStruct(fine_in.shape, BF),
-            jax.ShapeDtypeStruct((par_lane, k, kk), BF),
+            pltpu.VMEM(fine_in.shape, BF),
+            pltpu.VMEM((par_lane, k, kk), BF),
         ),
         in_specs=[hbm] * 15,
         out_specs=(vmem, vmem),

time: 43.1 us -> 43 us (level)
  local copies, waits for them, and re-layouts: 2.28 us -> 1.3 us
  Pallas kernels: 40 us -> 40.9 us
    unnamed x4 -> x2, local copies, waits for them, and re-layouts: 2.28 us -> 1.3 us
    pallas_call x1, Pallas kernels: 40 us -> 40.9 us  [body(): pl.pallas_call(functools.partial(tree_kernel, dims), out_shape=(pltpu.VME...]
where the time goes in v4:
time: 43 us; the launch traced here: 42.9 us
  Pallas kernels  40.9 us (95%)
  local copies, waits for them, and re-layouts  1.3 us (3%)
  between operations  0.64 us (1%)
    pallas_call x1, Pallas kernels, body(): pl.pallas_call(functools.partial(tree_kernel, dims), out_shape=(pltpu.VME...  40.9 us
    unnamed x2, local copies, waits for them, and re-layouts  1.3 us

profile of v4, /device:TPU:0, one launch (start us, length us, event | category | flops | bytes accessed | tf_op | source)
XLA Modules:
  0.0 42.9 jit_solution(14152469303669070742)
XLA Ops:
  0.6 40.9 %shard_map.158 = (bf16[2,16,16,256]{3,2,1,0:T(8,128)(2,1)S(1)}, bf16[1,16,256]{2,1,0:T(8,128)(2,1)S(1)}) custom-call(bf16[2,16,16,256]{3,2,1,0:T(8,128)(2,1)} %fine_hbm.1, s32[2]{0:T(128)} %bitcast.1, s32[2,16,16]{2,1,0:T(8,128)} %refs_hbm.1, s32[2,16,16]{2,1,0:T(8,128)} %codes_hbm.1, s32[2,16,16]{2,1,0:T(8,128)} %mask_hbm.1, s32[2,1,64]{2,1,0:T(1,128)} %slots_hbm.1, ...), custom_call_target="tpu_custom_call" | custom-call | tf_op jit(solution)/shard_map/pallas_call | solution.py:529
  41.6 0.7 %copy.19 = bf16[2,16,16,256]{3,2,1,0:T(8,128)(2,1)} copy(bf16[2,16,16,256]{3,2,1,0:T(8,128)(2,1)S(1)} %get-tuple-element.2) | data formatting | bytes 524288
  42.3 0.6 %copy.20 = bf16[1,16,256]{2,1,0:T(8,128)(2,1)} copy(bf16[1,16,256]{2,1,0:T(8,128)(2,1)S(1)} %get-tuple-element.3) | data formatting | bytes 16384

commit v5 on v4

--- a/solution.py
+++ b/solution.py
@@ -215,18 +215,18 @@
         pltpu.make_async_copy(src, dst, in_sems.at[i])
         for i, (src, dst) in enumerate(
             [
-                (ops_y_hbm, ops_y_ref),
-                (ops_z_hbm, ops_z_ref),
-                (slots_hbm, slots_ref),
-                (fine_hbm.at[0], own_0),
                 (filters_hbm, filters_ref),
                 (fine_hbm.at[1], own_1),
                 (child_hbm, child_ref),
                 (parent_hbm, parent_ref),
+                (slots_hbm, slots_ref),
+                (fine_hbm.at[0], own_0),
                 (crefs_hbm, crefs_ref),
                 (ccodes_hbm, ccodes_ref),
                 (cmask_hbm, cmask_ref),
                 (ops_x_hbm, ops_x_ref),
+                (ops_y_hbm, ops_y_ref),
+                (ops_z_hbm, ops_z_ref),
                 (refs_hbm, refs_ref),
                 (codes_hbm, codes_ref),
                 (mask_hbm, mask_ref),
@@ -293,23 +293,13 @@
         pool[level][slot + n_dev * cap] = jnp.zeros((k, k * k), BF)
         pool[level][pl.ds(0, slot)] = own[level][...]
 
-    for fetch in fetches[:2]:
-        fetch.wait()
-    build_tables(2, ops_y_ref, ops_z_ref, kr.at[2], k, terms)
     pl.semaphore_wait(barrier, n_dev - 1)
     send_mate(slots_hbm, slots_vec, 2)
     send_mate(fine_hbm.at[0], mate_0, 0)
-    send_mate(fine_hbm.at[1], mate_1, 1)
-    for fetch in fetches[2:4]:
-        fetch.wait()
-    send_fine(0, me, own_0, slots_ref, packed_own)
-
-    for fetch in fetches[4:8]:
+
+    for fetch in fetches[:4]:
         fetch.wait()
     build_filters(filters_ref, hk, k)
-    await_bytes(slots_vec, recv_mate.at[2])
-    slots_copy = pltpu.make_async_copy(slots_vec, mate_slots, in_sems.at[2])
-    slots_copy.start()
     both = jnp.concatenate([filters_ref[0], filters_ref[1]], axis=0)
     for b in range(slot):
         lifted = dot_nn(both, own_1[b])
@@ -326,7 +316,7 @@
         total = jnp.zeros((k, k * k), F32)
         for b in range(slot):
             total = total + jnp.where(parent_ref[b] == t, terms_up[b * k : (b + 1) * k], 0.0)
-        partial[t // par_lane, t % par_lane] = total
+        partial[t // par_lane, t % par_lane] = total.astype(BF)
 
     def send_partial(i, carry):
         to = lax.rem(lane + i, n_lane)
@@ -341,33 +331,22 @@
         return carry
 
     lax.fori_loop(1, n_lane, send_partial, 0)
+    send_mate(fine_hbm.at[1], mate_1, 1)
+    await_bytes(slots_vec, recv_mate.at[2])
+    slots_copy = pltpu.make_async_copy(slots_vec, mate_slots, in_sems.at[16])
+    slots_copy.start()
+    for fetch in fetches[4:6]:
+        fetch.wait()
+    send_fine(0, me, own_0, slots_ref, packed_own)
     slots_copy.wait()
     pass_mate(0)
-    send_fine(1, me, own_1, slots_ref, packed_own)
 
     rs_buf[lane] = partial[lane]
     coarse_all[n_dev * par_lane] = jnp.zeros((k, k * k), BF)
-    keep_own(0)
-    keep_own(1)
-    for fetch in fetches[8:]:
-        fetch.wait()
-    fill_index(crefs_ref[...], ccodes_ref[...], cmask_ref[...], n_dev * par_lane, cidx_vec, ...)
-    for level in range(2):
-        fill_index(
-            refs_ref[level], codes_ref[level], mask_ref[level], slot + n_dev * cap, idx_vec, level
-        )
-    table_copies = [
-        pltpu.make_async_copy(cidx_vec, cidx_ref, in_sems.at[0]),
-        pltpu.make_async_copy(idx_vec, idx_ref, in_sems.at[1]),
-    ]
-    for copy in table_copies:
-        copy.start()
-    build_tables(0, ops_y_ref, ops_z_ref, kr.at[0], k, terms)
-
     await_bytes(rs_buf.at[pl.ds(0, n_lane - 1)], recv_rs)
-    total = rs_buf[0]
+    total = rs_buf[0].astype(F32)
     for t in range(1, n_lane):
-        total = total + rs_buf[t]
+        total = total + rs_buf[t].astype(F32)
     coarse_all[pl.ds(me * par_lane, par_lane)] = total.astype(BF)
 
     odd = lax.rem(grp, 2)
@@ -387,6 +366,25 @@
         return carry
 
     lax.fori_loop(1, half, send_coarse, 0)
+    send_fine(1, me, own_1, slots_ref, packed_own)
+    keep_own(0)
+    keep_own(1)
+    for fetch in fetches[6:]:
+        fetch.wait()
+    fill_index(crefs_ref[...], ccodes_ref[...], cmask_ref[...], n_dev * par_lane, cidx_vec, ...)
+    for level in range(2):
+        fill_index(
+            refs_ref[level], codes_ref[level], mask_ref[level], slot + n_dev * cap, idx_vec, level
+        )
+    table_copies = [
+        pltpu.make_async_copy(cidx_vec, cidx_ref, in_sems.at[17]),
+        pltpu.make_async_copy(idx_vec, idx_ref, in_sems.at[18]),
+    ]
+    for copy in table_copies:
+        copy.start()
+    for level in (0, 2):
+        build_tables(level, ops_y_ref, ops_z_ref, kr.at[level], k, terms)
+
     pass_mate(1)
     build_tables(1, ops_y_ref, ops_z_ref, kr.at[1], k, terms)
     for copy in table_copies:
@@ -563,15 +561,15 @@
             pltpu.VMEM((slot, k, kk), BF),
             pltpu.VMEM(send_slots.shape, int32),
             pltpu.SMEM(send_slots.shape, int32),
-            pltpu.VMEM((n_lane, par_lane, k, kk), F32),
-            pltpu.VMEM((n_lane, par_lane, k, kk), F32),
+            pltpu.VMEM((n_lane, par_lane, k, kk), BF),
+            pltpu.VMEM((n_lane, par_lane, k, kk), BF),
             pltpu.VMEM((n_dev * par_lane + 1, k, kk), BF),
             pltpu.VMEM((n_lane, par_lane, k, kk), BF),
             pltpu.VMEM((4, kk, kk), BF),
             pltpu.VMEM((3, terms, PLANES * kk, kk), BF),
             pltpu.VMEM((terms, slot * k, PLANES * kk), BF),
             pltpu.VMEM((4, slot * k, kk), BF),
-            dma((16,)),
+            dma((20,)),
             dma,
             dma,
             dma,

time: 43 us -> 40 us (0.930)
  Pallas kernels: 40.9 us -> 37.9 us
    pallas_call x1, Pallas kernels: 40.9 us -> 37.9 us  [body(): pl.pallas_call(functools.partial(tree_kernel, dims), out_shape=(pltpu.VME...]
where the time goes in v5:
time: 40 us; the launch traced here: 39.8 us
  Pallas kernels  37.9 us (95%)
  local copies, waits for them, and re-layouts  1.3 us (3%)
  between operations  0.64 us (2%)
    pallas_call x1, Pallas kernels, body(): pl.pallas_call(functools.partial(tree_kernel, dims), out_shape=(pltpu.VME...  37.9 us
    unnamed x2, local copies, waits for them, and re-layouts  1.3 us

profile of v5, /device:TPU:0, one launch (start us, length us, event | category | flops | bytes accessed | tf_op | source)
XLA Modules:
  0.0 39.8 jit_solution(7826304220021358001)
XLA Ops:
  0.6 37.9 %shard_map.158 = (bf16[2,16,16,256]{3,2,1,0:T(8,128)(2,1)S(1)}, bf16[1,16,256]{2,1,0:T(8,128)(2,1)S(1)}) custom-call(bf16[2,16,16,256]{3,2,1,0:T(8,128)(2,1)} %fine_hbm.1, s32[2]{0:T(128)} %bitcast.1, s32[2,16,16]{2,1,0:T(8,128)} %refs_hbm.1, s32[2,16,16]{2,1,0:T(8,128)} %codes_hbm.1, s32[2,16,16]{2,1,0:T(8,128)} %mask_hbm.1, s32[2,1,64]{2,1,0:T(1,128)} %slots_hbm.1, ...), custom_call_target="tpu_custom_call" | custom-call | tf_op jit(solution)/shard_map/pallas_call | solution.py:527
  38.5 0.7 %copy.19 = bf16[2,16,16,256]{3,2,1,0:T(8,128)(2,1)} copy(bf16[2,16,16,256]{3,2,1,0:T(8,128)(2,1)S(1)} %get-tuple-element.2) | data formatting | bytes 524288
  39.2 0.6 %copy.20 = bf16[1,16,256]{2,1,0:T(8,128)(2,1)} copy(bf16[1,16,256]{2,1,0:T(8,128)(2,1)S(1)} %get-tuple-element.3) | data formatting | bytes 16384

commit v6 on v5

--- a/solution.py
+++ b/solution.py
@@ -178,6 +178,7 @@
     kr,
     s_buf,
     wide,
+    drop_buf,
     in_sems,
     send_rs,
     recv_rs,
@@ -293,13 +294,14 @@
         pool[level][slot + n_dev * cap] = jnp.zeros((k, k * k), BF)
         pool[level][pl.ds(0, slot)] = own[level][...]
 
+    fetches[0].wait()
+    build_filters(filters_ref, hk, k)
     pl.semaphore_wait(barrier, n_dev - 1)
     send_mate(slots_hbm, slots_vec, 2)
     send_mate(fine_hbm.at[0], mate_0, 0)
 
-    for fetch in fetches[:4]:
+    for fetch in fetches[1:4]:
         fetch.wait()
-    build_filters(filters_ref, hk, k)
     both = jnp.concatenate([filters_ref[0], filters_ref[1]], axis=0)
     for b in range(slot):
         lifted = dot_nn(both, own_1[b])
@@ -316,7 +318,7 @@
         total = jnp.zeros((k, k * k), F32)
         for b in range(slot):
             total = total + jnp.where(parent_ref[b] == t, terms_up[b * k : (b + 1) * k], 0.0)
-        partial[t // par_lane, t % par_lane] = total.astype(BF)
+        partial[t // par_lane, t % par_lane] = total
 
     def send_partial(i, carry):
         to = lax.rem(lane + i, n_lane)
@@ -344,9 +346,9 @@
     rs_buf[lane] = partial[lane]
     coarse_all[n_dev * par_lane] = jnp.zeros((k, k * k), BF)
     await_bytes(rs_buf.at[pl.ds(0, n_lane - 1)], recv_rs)
-    total = rs_buf[0].astype(F32)
+    total = rs_buf[0]
     for t in range(1, n_lane):
-        total = total + rs_buf[t].astype(F32)
+        total = total + rs_buf[t]
     coarse_all[pl.ds(me * par_lane, par_lane)] = total.astype(BF)
 
     odd = lax.rem(grp, 2)
@@ -386,9 +388,6 @@
         build_tables(level, ops_y_ref, ops_z_ref, kr.at[level], k, terms)
 
     pass_mate(1)
-    build_tables(1, ops_y_ref, ops_z_ref, kr.at[1], k, terms)
-    for copy in table_copies:
-        copy.wait()
 
     await_bytes(coarse_all.at[pl.ds(0, (half - 1) * par_lane)], recv_ag)
     for pair in range(n_grp // 2):
@@ -402,12 +401,9 @@
             device_id_type=MESH,
         ).start()
 
-    await_bytes(pool_0.at[pl.ds(0, (n_dev - 2) * cap)], recv_fine.at[0])
-    result = fine_operator(0, pool_0, idx_ref, ops_x_ref, kr.at[0], s_buf, slot, k, terms)
-    for b in range(slot):
-        value = jnp.where(b < counts_ref[0], result[b * k : (b + 1) * k], 0.0)
-        out_ref[0, b] = value.astype(BF)
-
+    build_tables(1, ops_y_ref, ops_z_ref, kr.at[1], k, terms)
+    for copy in table_copies:
+        copy.wait()
     rows_mat = build_rows(2, ops_x_ref, 1, k, terms)
     await_bytes(coarse_all.at[pl.ds(0, half * par_lane)], recv_pass)
     for b in range(par_lane):
@@ -433,15 +429,22 @@
 
     lax.fori_loop(1, n_lane, send_result, 0)
 
-    await_bytes(pool_1.at[pl.ds(0, (n_dev - 2) * cap)], recv_fine.at[1])
-    result = fine_operator(1, pool_1, idx_ref, ops_x_ref, kr.at[1], s_buf, slot, k, terms)
+    await_bytes(pool_0.at[pl.ds(0, (n_dev - 2) * cap)], recv_fine.at[0])
+    result = fine_operator(0, pool_0, idx_ref, ops_x_ref, kr.at[0], s_buf, slot, k, terms)
+    for b in range(slot):
+        value = jnp.where(b < counts_ref[0], result[b * k : (b + 1) * k], 0.0)
+        out_ref[0, b] = value.astype(BF)
+
     await_bytes(group_all.at[pl.ds(0, n_lane - 1)], recv_co)
     correction = drop(
         group_all, parent_ref, child_ref, filters_ref, hk, wide, slot, par_lane, k
     )
+    drop_buf[...] = correction
+    await_bytes(pool_1.at[pl.ds(0, (n_dev - 2) * cap)], recv_fine.at[1])
+    result = fine_operator(1, pool_1, idx_ref, ops_x_ref, kr.at[1], s_buf, slot, k, terms)
     for b in range(slot):
         value = jnp.where(b < counts_ref[1], result[b * k : (b + 1) * k], 0.0)
-        out_ref[1, b] = (value + correction[b * k : (b + 1) * k]).astype(BF)
+        out_ref[1, b] = (value + drop_buf[b * k : (b + 1) * k, :]).astype(BF)
 
     await_bytes(rs_buf.at[pl.ds(0, n_lane - 1)], send_rs)
     await_bytes(coarse_all.at[pl.ds(0, (half - 1) * par_lane)], send_ag)
@@ -561,14 +564,15 @@
             pltpu.VMEM((slot, k, kk), BF),
             pltpu.VMEM(send_slots.shape, int32),
             pltpu.SMEM(send_slots.shape, int32),
-            pltpu.VMEM((n_lane, par_lane, k, kk), BF),
-            pltpu.VMEM((n_lane, par_lane, k, kk), BF),
+            pltpu.VMEM((n_lane, par_lane, k, kk), F32),
+            pltpu.VMEM((n_lane, par_lane, k, kk), F32),
             pltpu.VMEM((n_dev * par_lane + 1, k, kk), BF),
             pltpu.VMEM((n_lane, par_lane, k, kk), BF),
             pltpu.VMEM((4, kk, kk), BF),
             pltpu.VMEM((3, terms, PLANES * kk, kk), BF),
             pltpu.VMEM((terms, slot * k, PLANES * kk), BF),
             pltpu.VMEM((4, slot * k, kk), BF),
+            pltpu.VMEM((slot * k, kk), F32),
             dma((20,)),
             dma,
             dma,

time: 40 us -> 42.7 us (1.068)
  Pallas kernels: 37.9 us -> 40.6 us
    pallas_call x1, Pallas kernels: 37.9 us -> 40.6 us  [body(): pl.pallas_call(functools.partial(tree_kernel, dims), out_shape=(pltpu.VME...]
where the time goes in v6:
time: 42.7 us; the launch traced here: 42.5 us
  Pallas kernels  40.6 us (95%)
  local copies, waits for them, and re-layouts  1.3 us (3%)
  between operations  0.64 us (1%)
    pallas_call x1, Pallas kernels, body(): pl.pallas_call(functools.partial(tree_kernel, dims), out_shape=(pltpu.VME...  40.6 us
    unnamed x2, local copies, waits for them, and re-layouts  1.3 us

profile of v6, /device:TPU:0, one launch (start us, length us, event | category | flops | bytes accessed | tf_op | source)
XLA Modules:
  0.0 42.5 jit_solution(10579240338541785267)
XLA Ops:
  0.6 40.6 %shard_map.158 = (bf16[2,16,16,256]{3,2,1,0:T(8,128)(2,1)S(1)}, bf16[1,16,256]{2,1,0:T(8,128)(2,1)S(1)}) custom-call(bf16[2,16,16,256]{3,2,1,0:T(8,128)(2,1)} %fine_hbm.1, s32[2]{0:T(128)} %bitcast.1, s32[2,16,16]{2,1,0:T(8,128)} %refs_hbm.1, s32[2,16,16]{2,1,0:T(8,128)} %codes_hbm.1, s32[2,16,16]{2,1,0:T(8,128)} %mask_hbm.1, s32[2,1,64]{2,1,0:T(1,128)} %slots_hbm.1, ...), custom_call_target="tpu_custom_call" | custom-call | tf_op jit(solution)/shard_map/pallas_call | solution.py:530
  41.2 0.7 %copy.19 = bf16[2,16,16,256]{3,2,1,0:T(8,128)(2,1)} copy(bf16[2,16,16,256]{3,2,1,0:T(8,128)(2,1)S(1)} %get-tuple-element.2) | data formatting | bytes 524288
  41.9 0.6 %copy.20 = bf16[1,16,256]{2,1,0:T(8,128)(2,1)} copy(bf16[1,16,256]{2,1,0:T(8,128)(2,1)S(1)} %get-tuple-element.3) | data formatting | bytes 16384
